TPU v7x, 256 devices: a whole 4x4x8 slice. The times are simulated.
256 devices in a mesh: band: 4 (over x), space: 64 (over z, y, core).
Axes of the slice: x: 4, y: 4, z: 8, core: 2. Of those that a mesh axis runs over, the one named last changes fastest.
Arguments:
- lanczos_now: float32 [2, 4, 1048576], P(None, 'band', 'space'), may hold values from -16 to 16
- lanczos_prev: float32 [2, 4, 1048576], P(None, 'band', 'space'), may hold values from -6 to 6
- beta_prev: float32 [1], replicated, may hold values from 0.5 to 1.5
- orbitals: float32 [2, 4, 192, 192, 192], P(None, 'band', 'space'), may hold values from -6 to 6
- band_energy: float32 [4], P('band'), may hold values from -2 to -0.5
- occupied: float32 [2, 64, 1048576], P(None, 'band', 'space'), may hold values from -0.0034526698 to 0.0034526698
- local_pot: float32 [192, 192, 192], P('space'), may hold values from -1 to 1
- xc_kernel: float32 [192, 192, 192], P('space'), may hold values from -1.5 to -0.3
- miller: int32 [3, 1048576], P(None, 'space'), may hold values from 0 to 191, as said below
Outputs:
- lanczos_next: float32 [2, 4, 1048576], P(None, 'band', 'space')
- coefficients: float32 [1, 2], replicated
- potential: float32 [192, 192, 192], P('space')
Inputs may be any that keep to these rules, and one draw needn't show every extreme that they name: `miller`: each column is a distinct grid point; the plane waves of the k-th block of 16384 columns have their second index in [k * 192 / 64, (k + 1) * 192 / 64).
All inputs are finite; a program needn't handle non-finite values.
Results may differ from a plain program's by a relative error of at most 0.0001.
Values sent between devices are 32-bit elements; how exact they have to be, the bound alone decides.
A program may use at most 64 MiB of HBM per device.

v0:
```python
import math

import jax
import jax.numpy as jnp
from jax import lax
from jax.sharding import PartitionSpec as P

HIGH = lax.Precision.HIGHEST
KINETIC = 8.0
HARTREE = 4.0


def signed(indices, length):
    return jnp.where(indices < length // 2, indices, indices - length)


def tables(length):
    indices = jnp.arange(length, dtype=jnp.int32)
    product = indices[:, None] * indices[None, :] % length
    angles = product.astype(jnp.float32) * (2.0 * math.pi / length)
    factor = 1.0 / math.sqrt(length)
    return (jnp.cos(angles) * factor, jnp.sin(angles) * factor)


def along_dim(values, matrix, dimension):
    shifted = jnp.moveaxis(values, dimension, -1)
    product = jnp.dot(shifted, matrix, precision=HIGH)
    return jnp.moveaxis(product, -1, dimension)


def transform(real_part, imag_part, dimension, sign):
    cosine, sine_part = tables(real_part.shape[dimension])
    new_real = along_dim(real_part, cosine, dimension) - sign * along_dim(
        imag_part, sine_part, dimension
    )
    new_imag = along_dim(imag_part, cosine, dimension) + sign * along_dim(
        real_part, sine_part, dimension
    )
    return (new_real, new_imag)


def transform_real(values, dimension, sign):
    cosine, sine_part = tables(values.shape[dimension])
    return (along_dim(values, cosine, dimension), sign * along_dim(values, sine_part, dimension))


def coulomb_factor(first_index, second_index, third_index, length):
    first_signed = signed(first_index, length)
    second_signed = signed(second_index, length)
    third_signed = signed(third_index, length)
    squared = (
        first_signed * first_signed + second_signed * second_signed + third_signed * third_signed
    )
    return jnp.where(squared > 0, HARTREE / jnp.maximum(squared, 1).astype(jnp.float32), 0.0)


def per_device(
    lanczos_now,
    lanczos_prev,
    beta_prev,
    orbitals,
    band_energy,
    occupied,
    local_pot,
    xc_kernel,
    miller,
):
    spaces = lax.axis_size("space")
    groups = lax.axis_size("band")
    planes = local_pot.shape[0]
    length = local_pot.shape[1]
    band_dev = lanczos_now.shape[1]
    wave_count = lanczos_now.shape[2]
    entries = float(2 * band_dev * groups * wave_count * spaces)
    flat_size = length * planes * length
    first_index = miller[0]
    second_index = miller[1]
    third_index = miller[2]
    position = (first_index * planes + second_index % planes) * length + third_index
    first_signed = signed(first_index, length)
    second_signed = signed(second_index, length)
    third_signed = signed(third_index, length)
    squared_wave = (
        first_signed * first_signed + second_signed * second_signed + third_signed * third_signed
    )
    kinetic = KINETIC * squared_wave.astype(jnp.float32) / float(length * length)
    space_start = lax.axis_index("space") * planes
    full_axis = jnp.arange(length, dtype=jnp.int32)
    plane_axis = jnp.arange(planes, dtype=jnp.int32)
    orbit_re = orbitals[0]
    orbit_im = orbitals[1]
    current_re = lanczos_now[0]
    current_im = lanczos_now[1]
    previous_re = lanczos_prev[0]
    previous_im = lanczos_prev[1]
    beta_value = beta_prev[0]

    def place(values):
        placed = jnp.zeros((band_dev, flat_size), jnp.float32).at[:, position].set(values)
        return placed.reshape(band_dev, length, planes, length)

    real_part, imag_part = transform(place(current_re), place(current_im), 3, 1.0)
    real_part, imag_part = transform(real_part, imag_part, 1, 1.0)
    operands = (
        lax.all_to_all(real_part, "space", split_axis=1, concat_axis=2, tiled=True),
        lax.all_to_all(imag_part, "space", split_axis=1, concat_axis=2, tiled=True),
    )
    field_re, field_im = transform(operands[0], operands[1], 2, 1.0)
    partial_value = 2.0 * jnp.sum(orbit_re * field_re + orbit_im * field_im, axis=0)
    density = lax.psum(partial_value, "band")
    real_part, imag_part = transform_real(density, 1, -1.0)
    real_part, imag_part = (
        lax.all_to_all(real_part, "space", split_axis=1, concat_axis=0, tiled=True),
        lax.all_to_all(imag_part, "space", split_axis=1, concat_axis=0, tiled=True),
    )
    real_part, imag_part = transform(real_part, imag_part, 0, -1.0)
    real_part, imag_part = transform(real_part, imag_part, 2, -1.0)
    factor = coulomb_factor(
        full_axis[:, None, None],
        (space_start + plane_axis)[None, :, None],
        full_axis[None, None, :],
        length,
    )
    real_part, imag_part = transform(factor * real_part, factor * imag_part, 2, 1.0)
    real_part, imag_part = transform(real_part, imag_part, 0, 1.0)
    real_part, imag_part = (
        lax.all_to_all(real_part, "space", split_axis=0, concat_axis=1, tiled=True),
        lax.all_to_all(imag_part, "space", split_axis=0, concat_axis=1, tiled=True),
    )
    real_part, imag_part = transform(real_part, imag_part, 1, 1.0)
    potential = real_part + xc_kernel * density
    mixed_re = local_pot * field_re + potential * orbit_re
    mixed_im = local_pot * field_im + potential * orbit_im
    mixed_re, mixed_im = transform(mixed_re, mixed_im, 2, -1.0)
    operands = (
        lax.all_to_all(mixed_re, "space", split_axis=2, concat_axis=1, tiled=True),
        lax.all_to_all(mixed_im, "space", split_axis=2, concat_axis=1, tiled=True),
    )
    part_re, part_im = transform(operands[0], operands[1], 1, -1.0)
    part_re, part_im = transform(part_re, part_im, 3, -1.0)
    count_rows = part_re.shape[0]
    wave_re = part_re.reshape(count_rows, flat_size)[:, position]
    wave_im = part_im.reshape(count_rows, flat_size)[:, position]
    diagonal_terms = kinetic[None, :] - band_energy[:, None]
    lifted_re = diagonal_terms * current_re + wave_re
    lifted_im = diagonal_terms * current_im + wave_im
    stacked = jnp.stack(
        [
            lax.all_gather(lifted_re, "band", axis=0, tiled=True),
            lax.all_gather(lifted_im, "band", axis=0, tiled=True),
        ]
    )
    prods = jnp.einsum("con,pvn->cpov", occupied, stacked, precision=HIGH)
    add_over_re = prods[0, 0] + prods[1, 1]
    add_over_im = prods[0, 1] - prods[1, 0]
    over_re = add_over_re
    over_im = add_over_im
    over_re, over_im = lax.psum((over_re, over_im), "space")
    prods = jnp.einsum("con,pov->cpvn", occupied, jnp.stack([over_re, over_im]), precision=HIGH)
    corr_re = prods[0, 0] - prods[1, 1]
    corr_im = prods[0, 1] + prods[1, 0]
    removed = lax.psum_scatter(
        jnp.stack([corr_re, corr_im], axis=1), "band", scatter_dimension=0, tiled=True
    )
    image_re, image_im, potential = (
        lifted_re - removed[:, 0],
        lifted_im - removed[:, 1],
        potential,
    )
    curve = lax.psum(jnp.sum(current_re * image_re + current_im * image_im), ("band", "space"))
    alpha_value = curve / entries
    rest_re = image_re - alpha_value * current_re - beta_value * previous_re
    rest_im = image_im - alpha_value * current_im - beta_value * previous_im
    square = lax.psum(jnp.sum(rest_re * rest_re + rest_im * rest_im), ("band", "space"))
    beta_new = jnp.sqrt(square / entries)
    current_re = rest_re / beta_new
    current_im = rest_im / beta_new
    rows_out = [jnp.stack([alpha_value, beta_new])]
    return (jnp.stack([current_re, current_im]), jnp.stack(rows_out), potential)


def solution(mesh):
    return jax.shard_map(
        per_device,
        mesh=mesh,
        in_specs=(
            P(None, "band", "space"),
            P(None, "band", "space"),
            P(),
            P(None, "band", "space", None, None),
            P("band"),
            P(None, "band", "space"),
            P("space", None, None),
            P("space", None, None),
            P(None, "space"),
        ),
        out_specs=(P(None, "band", "space"), P(), P("space", None, None)),
        check_vma=False,
    )
```

profile of v0, /device:TPU:1, one launch (start us, length us, event | category | flops | bytes accessed | tf_op | source)
XLA Modules:
  0.0 1056.4 jit_solution(18342940318168701248)
XLA Ops:
  10.5 60.4 %scatter_custom_fusion = f32[110592]{0:T(1024)S(1)} fusion(s32[16384]{0:T(1024)S(1)} %bitcast.457, f32[16384]{0:T(1024)S(1)} %bitcast.463, f32[]{:T(128)} %constant.100.clone.1), kind=kCustom, calls=%fused_computation.130 | custom fusion | bytes 442372 | tf_op jit(solution)/shard_map/scatter | solution.py:99
  72.7 61.8 %scatter_custom_fusion.1 = f32[110592]{0:T(1024)} fusion(s32[16384]{0:T(1024)S(1)} %bitcast.458, f32[16384]{0:T(1024)} %bitcast.462, f32[]{:T(128)} %constant.100.clone.1), kind=kCustom, calls=%fused_computation.128 | custom fusion | bytes 442880 | tf_op jit(solution)/shard_map/scatter | solution.py:99
  134.5 2.4 reshape.400
  136.9 2.5 fusion.70
  139.4 2.6 fusion.29
  142.0 1.9 fusion.136
  145.3 2.7 fusion.27
  148.0 2.1 copy.173
  150.1 13.7 %all-to-all-start = ((f32[1,192,3,192]{3,0,2,1:T(1,128)}), f32[1,192,3,192]{3,0,2,1:T(1,128)}, u32[]{:S(2)}, u32[]{:S(2)}) async-start(f32[1,192,3,192]{3,0,2,1:T(1,128)} %copy.173), calls=%async_computation | async-start | bytes 1179648 | tf_op jit(solution)/shard_map/all_to_all | solution.py:105
  163.8 1.9 fusion.132
  165.6 1.9 fusion.26
  168.8 13.8 %all-to-all-done = f32[1,192,3,192]{3,0,2,1:T(1,128)} async-done(((f32[1,192,3,192]{3,0,2,1:T(1,128)}), f32[1,192,3,192]{3,0,2,1:T(1,128)}, u32[]{:S(2)}, u32[]{:S(2)}) %all-to-all-start) | async-done | bytes 442400 | tf_op jit(solution)/shard_map/all_to_all | solution.py:105
  182.6 6.0 all-to-all-start.1
  188.6 2.2 fusion.340
  192.6 2.5 copy.174
  195.1 2.0 copy.175
  197.1 3.3 fusion.60
  200.3 7.2 all-to-all-done.1
  207.5 2.3 copy.179
  209.8 2.0 copy.180
  211.8 2.5 fusion.62
  214.3 2.6 fusion.25
  220.2 43.2 %all-reduce.5.cloned.1.call-done = f32[3,192,192]{1,2,0:T(8,128)} async-done(((f32[3,192,192]{1,2,0:T(8,128)}), f32[3,192,192]{1,2,0:T(8,128)}) %all-reduce.5.cloned.1.call-update) | async-done | bytes 442384 | tf_op jit(solution)/shard_map/psum | solution.py:110
  263.5 2.5 fusion.23
  267.2 12.5 %all-to-all-start.3 = ((f32[3,192,192]{2,0,1:T(4,128)}), f32[3,192,192]{2,0,1:T(4,128)S(1)}, u32[]{:S(2)}, u32[]{:S(2)}) async-start(f32[3,192,192]{2,0,1:T(4,128)} %copy.188), calls=%async_computation.3 | async-start | bytes 1572864 | tf_op jit(solution)/shard_map/all_to_all | solution.py:114
  279.8 2.2 convolution_bitcast_fusion.1
  282.0 2.3 copy.183
  284.2 18.3 %all-to-all-done.3 = f32[3,192,192]{2,0,1:T(4,128)S(1)} async-done(((f32[3,192,192]{2,0,1:T(4,128)}), f32[3,192,192]{2,0,1:T(4,128)S(1)}, u32[]{:S(2)}, u32[]{:S(2)}) %all-to-all-start.3) | async-done | bytes 442400 | tf_op jit(solution)/shard_map/all_to_all | solution.py:114
  302.5 6.8 all-to-all-start.2
  312.1 2.8 fusion.51
  314.9 16.7 %all-to-all-done.2 = f32[3,192,192]{2,0,1:T(4,128)} async-done(((f32[3,192,192]{2,0,1:T(4,128)}), f32[3,192,192]{2,0,1:T(4,128)}, u32[]{:S(2)}, u32[]{:S(2)}) %all-to-all-start.2) | async-done | bytes 442400 | tf_op jit(solution)/shard_map/all_to_all | solution.py:113
  335.3 2.0 fusion.55
  337.3 3.1 fusion.21
  341.8 2.0 fusion.22
  358.7 6.4 all-to-all-start.5
  369.3 18.5 %all-to-all-done.5 = f32[192,3,192]{2,1,0:T(4,128)} async-done(((f32[192,3,192]{2,1,0:T(4,128)}), f32[192,3,192]{2,1,0:T(4,128)}, u32[]{:S(2)}, u32[]{:S(2)}) %all-to-all-start.5) | async-done | bytes 442400 | tf_op jit(solution)/shard_map/all_to_all | solution.py:128
  387.8 6.2 all-to-all-start.4
  395.1 2.2 copy.211
  397.3 2.1 copy.209
  402.0 14.8 %all-to-all-done.4 = f32[192,3,192]{2,1,0:T(4,128)S(1)} async-done(((f32[192,3,192]{2,1,0:T(4,128)}), f32[192,3,192]{2,1,0:T(4,128)S(1)}, u32[]{:S(2)}, u32[]{:S(2)}) %all-to-all-start.4) | async-done | bytes 442400 | tf_op jit(solution)/shard_map/all_to_all | solution.py:127
  420.9 4.7 bitcast_add_fusion
  427.0 2.2 fusion.10
  429.3 2.1 copy.216
  431.3 6.4 all-to-all-start.7
  441.8 14.9 %all-to-all-done.7 = f32[1,3,192,192]{3,0,1,2:T(1,128)} async-done(((f32[1,3,192,192]{3,0,1,2:T(1,128)}), f32[1,3,192,192]{3,0,1,2:T(1,128)}, u32[]{:S(2)}, u32[]{:S(2)}) %all-to-all-start.7) | async-done | bytes 442400 | tf_op jit(solution)/shard_map/all_to_all | solution.py:137
  456.7 6.0 all-to-all-start.6
  467.6 2.2 fusion.39
  469.8 12.0 %all-to-all-done.6 = f32[1,3,192,192]{3,0,1,2:T(1,128)S(1)} async-done(((f32[1,3,192,192]{3,0,1,2:T(1,128)}), f32[1,3,192,192]{3,0,1,2:T(1,128)S(1)}, u32[]{:S(2)}, u32[]{:S(2)}) %all-to-all-start.6) | async-done | bytes 442400 | tf_op jit(solution)/shard_map/all_to_all | solution.py:136
  487.1 2.7 fusion.6
  489.8 1.9 fusion.113
  493.1 2.7 fusion.116
  495.8 1.9 fusion.3
  500.6 3.1 fusion.4
  506.7 90.5 %gather_fusion.1 = f32[16384]{0:T(1024)S(1)} fusion(f32[110592]{0:T(1024)S(1)} %reshape.425, s32[16384]{0:T(1024)S(1)} %broadcast_clamp_fusion), kind=kCustom, calls=%fused_computation.1 | custom fusion | bytes 196608 | tf_op jit(solution)/shard_map/gather | solution.py:143
  597.2 90.5 %gather_fusion = f32[16384]{0:T(1024)S(1)} fusion(f32[110592]{0:T(1024)S(1)} %reshape.415, s32[16384]{0:T(1024)S(1)} %broadcast_clamp_fusion), kind=kCustom, calls=%fused_computation | custom fusion | bytes 196608 | tf_op jit(solution)/shard_map/gather | solution.py:142
  688.3 9.4 all-gather
  697.8 9.4 all-gather.1
  707.4 8.0 fusion.30
  715.4 129.7 %all-reduce.1 = (f32[1,16,4]{1,2,0:T(4,128)S(1)}, f32[1,16,4]{1,2,0:T(4,128)S(1)}) all-reduce(f32[1,16,4]{1,2,0:T(4,128)S(1)} %get-tuple-element.29, f32[1,16,4]{1,2,0:T(4,128)S(1)} %get-tuple-element.28), channel_id=1, replica_groups=mesh['band'=4,'space'=64] {'space'}, use_global_device_ids=true, to_apply=%region_4.5 | all-reduce | flops 128 | bytes 1024 | tf_op jit(solution)/shard_map/psum | solution.py:158
  849.4 39.8 %all-reduce.7.cloned.1.call-done = f32[4,2,16384]{2,1,0:T(2,128)} async-done(((f32[4,2,16384]{2,1,0:T(2,128)}), f32[4,2,16384]{2,1,0:T(2,128)}) %all-reduce.7.cloned.1.call-update) | async-done | bytes 524304
  889.3 2.4 fusion.155
  892.8 77.6 %psum.38 = f32[]{:T(128)} all-reduce(f32[]{:T(128)} %fusion.155), channel_id=1, replica_groups=mesh['band'=4,'space'=64] {'band','space'}, use_global_device_ids=true, to_apply=%region_7.8 | all-reduce | flops 1 | bytes 8 | tf_op jit(solution)/shard_map/psum | solution.py:170
  971.0 2.5 add_reduce_fusion
  973.5 73.7 %psum.39 = f32[]{:T(128)} all-reduce(f32[]{:T(128)} %get-tuple-element.17), channel_id=1, replica_groups=mesh['band'=4,'space'=64] {'band','space'}, use_global_device_ids=true, to_apply=%region_9.10 | all-reduce | flops 1 | bytes 8 | tf_op jit(solution)/shard_map/psum | solution.py:174
  (113 shorter events, 77.8 us)
Async XLA Ops:
  7.2 700.2 %copy-start = (f32[2,16,16384]{2,1,0:T(8,128)S(1)}, f32[2,16,16384]{2,1,0:T(8,128)}, u32[]{:S(2)}) copy-start(f32[2,16,16384]{2,1,0:T(8,128)} %param.14) | copy-start | bytes 6291460
  71.3 65.5 %copy-start.10 = (f32[192,3,192]{2,1,0:T(4,128)}, f32[192,3,192]{2,1,0:T(4,128)S(1)}, u32[]{:S(2)}) copy-start(f32[192,3,192]{2,1,0:T(4,128)S(1)} %reshape.399) | copy-start | bytes 1327108
  139.4 4.5 copy-start.11
  150.1 32.5 %all-to-all-start = ((f32[1,192,3,192]{3,0,2,1:T(1,128)}), f32[1,192,3,192]{3,0,2,1:T(1,128)}, u32[]{:S(2)}, u32[]{:S(2)}) async-start(f32[1,192,3,192]{3,0,2,1:T(1,128)} %copy.173), calls=%async_computation | async-start | bytes 1179648 | tf_op jit(solution)/shard_map/all_to_all | solution.py:105
  182.6 24.9 %all-to-all-start.1 = ((f32[1,192,3,192]{3,0,2,1:T(1,128)}), f32[1,192,3,192]{3,0,2,1:T(1,128)}, u32[]{:S(2)}, u32[]{:S(2)}) async-start(f32[1,192,3,192]{3,0,2,1:T(1,128)} %copy.178), calls=%async_computation.1 | async-start | bytes 1179648 | tf_op jit(solution)/shard_map/all_to_all | solution.py:106
  188.5 74.9 %all-reduce.5.cloned.1.call-start = ((), (), s32[]{:S(2)}) async-start(), calls=%async_computation.8 | async-start | bytes 1179648 | tf_op jit(solution)/shard_map/psum | solution.py:110
  191.0 27.4 %copy-start.4 = (f32[1,1,3,192,192]{3,4,2,1,0:T(8,128)}, f32[1,1,3,192,192]{3,4,2,1,0:T(8,128)S(1)}, u32[]{:S(2)}) copy-start(f32[1,1,3,192,192]{3,4,2,1,0:T(8,128)S(1)} %copy.270) | copy-start | bytes 1327108
  192.6 25.8 %copy-start.5 = (f32[1,1,3,192,192]{3,4,2,1,0:T(8,128)}, f32[1,1,3,192,192]{3,4,2,1,0:T(8,128)S(1)}, u32[]{:S(2)}) copy-start(f32[1,1,3,192,192]{3,4,2,1,0:T(8,128)S(1)} %copy.271) | copy-start | bytes 1327108
  211.8 5.2 copy-start.8
  217.0 1.4 copy-start.1
  218.4 0.8 copy-start.2
  263.5 16.3 %copy-start.3 = (f32[3,192,192]{1,2,0:T(8,128)S(1)}, f32[3,192,192]{1,2,0:T(8,128)}, u32[]{:S(2)}) copy-start(f32[3,192,192]{1,2,0:T(8,128)} %all-reduce.5.cloned.1.call-done) | copy-start | bytes 1327108
  267.2 35.3 %all-to-all-start.3 = ((f32[3,192,192]{2,0,1:T(4,128)}), f32[3,192,192]{2,0,1:T(4,128)S(1)}, u32[]{:S(2)}, u32[]{:S(2)}) async-start(f32[3,192,192]{2,0,1:T(4,128)} %copy.188), calls=%async_computation.3 | async-start | bytes 1572864 | tf_op jit(solution)/shard_map/all_to_all | solution.py:114
  302.5 29.1 %all-to-all-start.2 = ((f32[3,192,192]{2,0,1:T(4,128)}), f32[3,192,192]{2,0,1:T(4,128)}, u32[]{:S(2)}, u32[]{:S(2)}) async-start(f32[3,192,192]{2,0,1:T(4,128)} %copy.183), calls=%async_computation.2 | async-start | bytes 1572864 | tf_op jit(solution)/shard_map/all_to_all | solution.py:113
  358.7 29.1 %all-to-all-start.5 = ((f32[192,3,192]{2,1,0:T(4,128)}), f32[192,3,192]{2,1,0:T(4,128)}, u32[]{:S(2)}, u32[]{:S(2)}) async-start(f32[192,3,192]{2,1,0:T(4,128)} %copy.207), calls=%async_computation.5 | async-start | bytes 1572864 | tf_op jit(solution)/shard_map/all_to_all | solution.py:128
  366.6 27.5 %copy-start.15 = (f32[3,192,192]{2,1,0:T(8,128)S(1)}, f32[3,192,192]{2,1,0:T(8,128)}, u32[]{:S(2)}) copy-start(f32[3,192,192]{2,1,0:T(8,128)} %param.15) | copy-start | bytes 1327108
  387.8 29.0 %all-to-all-start.4 = ((f32[192,3,192]{2,1,0:T(4,128)}), f32[192,3,192]{2,1,0:T(4,128)S(1)}, u32[]{:S(2)}, u32[]{:S(2)}) async-start(f32[192,3,192]{2,1,0:T(4,128)} %copy.199), calls=%async_computation.4 | async-start | bytes 1572864 | tf_op jit(solution)/shard_map/all_to_all | solution.py:127
  431.3 25.4 %all-to-all-start.7 = ((f32[1,3,192,192]{3,0,1,2:T(1,128)}), f32[1,3,192,192]{3,0,1,2:T(1,128)}, u32[]{:S(2)}, u32[]{:S(2)}) async-start(f32[1,3,192,192]{3,0,1,2:T(1,128)} %copy.216), calls=%async_computation.7 | async-start | bytes 1179648 | tf_op jit(solution)/shard_map/all_to_all | solution.py:137
  456.7 25.0 %all-to-all-start.6 = ((f32[1,3,192,192]{3,0,1,2:T(1,128)}), f32[1,3,192,192]{3,0,1,2:T(1,128)S(1)}, u32[]{:S(2)}, u32[]{:S(2)}) async-start(f32[1,3,192,192]{3,0,1,2:T(1,128)} %copy.212), calls=%async_computation.6 | async-start | bytes 1179648 | tf_op jit(solution)/shard_map/all_to_all | solution.py:136
  462.7 426.6 %all-reduce.7.cloned.1.call-start = ((), (), s32[]{:S(2)}) async-start(), calls=%async_computation.9 | async-start | bytes 1048576
  467.6 17.3 %copy-start.6 = (f32[1,192,3,192]{1,3,2,0:T(8,128)}, f32[1,192,3,192]{1,3,2,0:T(8,128)S(1)}, u32[]{:S(2)}) copy-start(f32[1,192,3,192]{1,3,2,0:T(8,128)S(1)} %copy.219) | copy-start | bytes 1327108
  484.9 0.8 copy-start.9
  487.1 4.6 copy-start.7
  597.2 90.6 %copy-start.13 = (f32[2,1,16384]{2,1,0:T(1,128)S(1)}, f32[2,1,16384]{2,1,0:T(1,128)}, u32[]{:S(2)}) copy-start(f32[2,1,16384]{2,1,0:T(1,128)} %param.9) | copy-start | bytes 393220
  597.2 90.6 %copy-start.14 = (s32[3,16384]{1,0:T(4,128)S(1)}, s32[3,16384]{1,0:T(4,128)}, u32[]{:S(2)}) copy-start(s32[3,16384]{1,0:T(4,128)} %param.17) | copy-start | bytes 589828
  846.7 2.2 copy-start.17
  846.8 44.9 %copy-start.12 = (f32[3,192,192]{1,2,0:T(8,128)S(1)}, f32[3,192,192]{1,2,0:T(8,128)}, u32[]{:S(2)}) copy-start(f32[3,192,192]{1,2,0:T(8,128)} %get-tuple-element.30) | copy-start | bytes 1327108
  846.8 124.2 %copy-start.16 = (f32[2,1,16384]{2,1,0:T(1,128)S(1)}, f32[2,1,16384]{2,1,0:T(1,128)}, u32[]{:S(2)}) copy-start(f32[2,1,16384]{2,1,0:T(1,128)} %param.10) | copy-start | bytes 393220
Sparse Core Ops, SparseCore 0:
  220.4 43.0 all-reduce.4
  848.3 40.8 all-reduce.6
where the time goes:
time: 1060 us
  local copies, waits for them, and re-layouts  368 us (35%)
  blocking collectives  300 us (28%)
  waiting for transfers between devices  199 us (19%)
  matrix products  97.3 us (9%)
  starting transfers between devices  64 us (6%)
  between operations  17.6 us (2%)
    psum x1, blocking collectives, per_device(): over_re, over_im = lax.psum((over_re, over_im), 'space')  130 us
    scatter x2, local copies, waits for them, and re-layouts, place(): jnp.zeros((band_dev, flat_size), jnp.float32).at[:, position].set(values)  122 us
    gather x1, local copies, waits for them, and re-layouts, per_device(): wave_im = part_im.reshape(count_rows, flat_size)[:, position]  90.5 us
    gather x1, local copies, waits for them, and re-layouts, per_device(): wave_re = part_re.reshape(count_rows, flat_size)[:, position]  90.5 us
    dot_general x44, matrix products, along_dim(): product = jnp.dot(shifted, matrix, precision=HIGH)  87.8 us
    psum x1, blocking collectives, per_device(): lax.psum(jnp.sum(current_re * image_re + current_im * image_im), ('band',...  77.6 us
    psum x1, blocking collectives, per_device(): lax.psum(jnp.sum(rest_re * rest_re + rest_im * rest_im), ('band', 'space'))  73.7 us
    psum x1, waiting for transfers between devices, per_device(): density = lax.psum(partial_value, 'band')  43.2 us
  transfers between devices with their start and end apart: 10, of which 10 were waited for; matrix products, arithmetic and copies ran while one was open for 4% of the time, Pallas kernels for 0%

commit v1 on v0

v1 whole, which is shorter than its diff:
```python
import math

import jax
import jax.numpy as jnp
import ml_dtypes
import numpy as np
from jax import lax
from jax.experimental import pallas as pl
from jax.experimental.pallas import tpu as pltpu
from jax.sharding import PartitionSpec as P

MESH = pl.DeviceIdType.MESH
F32 = jnp.float32
BF16 = jnp.bfloat16
KINETIC = 8.0
HARTREE = 4.0
N = 192
S = 64
G = 4
PL = 3
CELL = 9
HROWS = 4
QUART = N // G
HL = 512
TILE = 64
WAVES = 16384
PLACE = 2048
READ = 1024
BLOCK = 4096
STRIDE = 29
ENTRIES = float(2 * G * WAVES * S)


def split_np(table):
    high = table.astype(np.float32).astype(ml_dtypes.bfloat16)
    low = (table - high.astype(np.float64)).astype(np.float32).astype(ml_dtypes.bfloat16)
    return high, low


def left_table(table):
    high, low = split_np(table)
    return np.concatenate([high, high, low], axis=1)


def right_table(table):
    high, low = split_np(table)
    return np.concatenate([high, high, low], axis=0)


def make_tables():
    index = np.arange(N)
    angle = 2.0 * np.pi * (np.outer(index, index) % N) / N
    cosine = np.cos(angle) / math.sqrt(N)
    sine = np.sin(angle) / math.sqrt(N)
    order = np.concatenate([np.arange(S) * PL + part for part in range(PL)])
    re_lane = index // TILE * 128 + index % TILE
    im_lane = re_lane + TILE

    def lanes(sign):
        table = np.zeros((2 * N, 2 * N))
        table[np.ix_(re_lane, re_lane)] = cosine
        table[np.ix_(im_lane, re_lane)] = -sign * sine
        table[np.ix_(re_lane, im_lane)] = sign * sine
        table[np.ix_(im_lane, im_lane)] = cosine
        return table

    def rows(sign, row_order, column_order):
        both = [
            cosine[row_order][:, column_order],
            sign * sine[row_order][:, column_order],
        ]
        return left_table(np.concatenate(both, axis=1))

    cas = cosine + sine
    cas_in = np.zeros((2 * N, N))
    cas_in[re_lane] = cas
    cas_in[im_lane] = cas
    plus = lanes(1.0)
    return (
        np.stack([right_table(plus[t * 128 : (t + 1) * 128]) for t in range(3)]),
        right_table(lanes(-1.0)),
        rows(1.0, order, index),
        rows(1.0, index, order),
        rows(-1.0, order, index),
        rows(-1.0, index, order),
        right_table(cas_in),
        right_table(cas_in.T),
        left_table(cas[order]),
        left_table(cas[:, order]),
    )


def split(values):
    high = values.astype(BF16)
    low = (values - high.astype(F32)).astype(BF16)
    return high, low


def left(table_ref, values):
    high, low = split(values)
    stacked = jnp.concatenate([high, low, high], axis=0)
    return jnp.dot(table_ref[...], stacked, preferred_element_type=F32)


def right(values, table):
    high, low = split(values)
    stacked = jnp.concatenate([high, low, high], axis=1)
    return jnp.dot(stacked, table, preferred_element_type=F32)


def times_i(values):
    lane = lax.broadcasted_iota(jnp.int32, (values.shape[0], 128), 1)
    tiles = []
    for t in range(values.shape[1] // 128):
        turned = pltpu.roll(values[:, t * 128 : (t + 1) * 128], TILE, axis=1)
        tiles.append(jnp.where(lane < TILE, -turned, turned))
    return jnp.concatenate(tiles, axis=1)


def left_complex(table_ref, values):
    return left(table_ref, jnp.concatenate([values, times_i(values)], axis=0))


def signed(indices):
    return jnp.where(indices < N // 2, indices, indices - N)


def doubled(values):
    tiles = []
    for t in range(3):
        part = values[:, t * TILE : (t + 1) * TILE]
        tiles += [part, part]
    return jnp.concatenate(tiles, axis=1)


def body(*refs):
    now_ref, miller_ref, beta_ref, energy_ref = refs[:4]
    later = refs[4:19]
    rest_ref, scalars_ref, pot_ref = refs[19:22]
    held = refs[22:37]
    (
        prev_ref,
        orbit_ref,
        occ_ref,
        local_ref,
        xc_ref,
        lane_plus,
        lane_minus,
        a_plus,
        b_plus,
        b_minus,
        a_minus,
        cas_in,
        cas_out,
        cas_rows,
        cas_cols,
    ) = held
    (
        hot,
        acc,
        send1,
        recv1,
        fields,
        packed,
        w_send,
        w_recv,
        d_all,
        h_all,
        h_send1,
        h_recv1,
        h_send2,
        h_recv2,
        send2,
        recv2,
        table,
        lifted,
        over_send,
        over_recv,
        corr,
        corr_recv,
        sum_send1,
        sum_recv1,
        sum_send2,
        sum_recv2,
        sems,
        load_sems,
    ) = refs[37:]
    me = lax.axis_index("space")
    group = lax.axis_index("band")
    start = me * PL

    def load(at):
        return pltpu.make_async_copy(later[at], held[at], load_sems.at[at])

    for at in range(len(later)):
        load(at).start()

    barrier = pltpu.get_barrier_semaphore()

    def greet(step, carry):
        pl.semaphore_signal(
            barrier, inc=1, device_id={"space": lax.rem(me + step, S)}, device_id_type=MESH
        )
        return carry

    lax.fori_loop(1, S, greet, 0)
    for step in range(1, G):
        pl.semaphore_signal(
            barrier, inc=1, device_id={"band": lax.rem(group + step, G)}, device_id_type=MESH
        )

    def space_send(phase, source, target):
        def one(step, carry):
            peer = lax.rem(me + step * STRIDE, S)
            pltpu.make_async_remote_copy(
                src_ref=source(peer),
                dst_ref=target(me),
                send_sem=sems.at[phase, 0],
                recv_sem=sems.at[phase, 1],
                device_id={"space": peer},
                device_id_type=MESH,
            ).start()
            return carry

        lax.fori_loop(1, S, one, 0)

    def band_send(phase, source, target):
        for step in range(1, G):
            peer = lax.rem(group + step, G)
            pltpu.make_async_remote_copy(
                src_ref=source(peer),
                dst_ref=target(group),
                send_sem=sems.at[phase, 0],
                recv_sem=sems.at[phase, 1],
                device_id={"band": peer},
                device_id_type=MESH,
            ).start()

    def wait(phase, side, region):
        pltpu.make_async_copy(region, region, sems.at[phase, side]).wait()

    def part_chunk(ref, part):
        return lambda at: ref.at[pl.ds(part * S * CELL + at * CELL, CELL)]

    def chunk(ref):
        return lambda at: ref.at[pl.ds(at * HROWS, HROWS)]

    def keep(source, target, first, rows):
        own = pl.ds(first + me * rows, rows)
        target[own, :] = source[own, :]

    def cell_rows(part, m):
        return pl.ds(part * S * CELL + m, S, stride=CELL)

    def columns_at(step, size):
        return pl.ds(pl.multiple_of(step * size, size), size)

    def place(tile):
        def one(step, carry):
            columns = columns_at(step, PLACE)
            if tile == 0:
                row = (miller_ref[1:2, columns] - start) * N + miller_ref[0:1, columns]
                where = lax.broadcasted_iota(jnp.int16, (PL * N, PLACE), 0)
                hot[:, columns] = jnp.where(
                    where == row.astype(jnp.int16), BF16(1), BF16(0)
                )
            third = (miller_ref[2:3, columns] - tile * TILE).astype(jnp.int16)
            mask = lax.broadcasted_iota(jnp.int16, (TILE, PLACE), 0) == third
            parts = [jnp.where(mask, value, BF16(0)) for value in values_of(columns)]
            product = lax.dot_general(
                hot[:, columns],
                jnp.concatenate(parts, axis=0),
                (((1,), (1,)), ((), ())),
                preferred_element_type=F32,
            )
            acc[...] += product
            return carry

        acc[...] = jnp.zeros_like(acc)
        lax.fori_loop(0, WAVES // PLACE, one, 0)

    def values_of(columns):
        re_high, re_low = split(now_ref[0, 0:1, columns])
        im_high, im_low = split(now_ref[1, 0:1, columns])
        return re_high, im_high, re_low, im_low

    for t in range(3):
        place(t)
        placed = acc[:, 0:128] + acc[:, 128:256]
        if t == 0:
            load(7).wait()
        result = left_complex(
            a_plus, jnp.concatenate([placed[b * N : (b + 1) * N] for b in range(PL)], axis=1)
        )
        for r in range(PL):
            for b in range(PL):
                send1[cell_rows(t, r * PL + b), :] = result[
                    r * S : (r + 1) * S, b * 128 : (b + 1) * 128
                ]
        if t == 0:
            pl.semaphore_wait(barrier, S - 1 + G - 1)
        space_send(t, part_chunk(send1, t), part_chunk(recv1, t))
        keep(send1, recv1, t * S * CELL, CELL)

    for at in range(len(later)):
        if at != 7:
            load(at).wait()

    for r in range(PL):
        re = orbit_ref[0, 0, r]
        im = orbit_ref[1, 0, r]
        pieces = []
        for t in range(3):
            pieces += [re[:, t * TILE : (t + 1) * TILE], im[:, t * TILE : (t + 1) * TILE]]
        packed[r * N : (r + 1) * N] = jnp.concatenate(pieces, axis=1)

    every_chunk = pl.ds(0, (S - 1) * CELL)
    for t in range(3):
        wait(t, 1, recv1.at[every_chunk])
        values = jnp.concatenate(
            [
                jnp.concatenate([recv1[cell_rows(t, r * PL + b), :] for r in range(PL)], axis=1)
                for b in range(PL)
            ],
            axis=0,
        )
        result = left_complex(b_plus, values)
        result = jnp.concatenate([result[:, r * 128 : (r + 1) * 128] for r in range(PL)], axis=0)
        result = right(result, lane_plus[t])
        if t == 0:
            fields[...] = result
        else:
            fields[...] += result

    columns_of = right(2.0 * fields[...] * packed[...], cas_in[...])
    columns_of = [left(cas_rows, columns_of[r * N : (r + 1) * N]) for r in range(PL)]

    for g in range(G):
        pieces = []
        for r in range(PL):
            for b in range(PL):
                pieces.append(columns_of[r][b * S : (b + 1) * S, g * QUART : (g + 1) * QUART])
        pieces.append(jnp.zeros((S, HL - PL * PL * QUART), F32))
        w_send[g] = jnp.concatenate(pieces, axis=1)

    band_send(3, lambda peer: w_send.at[peer], lambda mine: w_recv.at[mine])
    w_recv[group] = w_send[group]
    wait(3, 1, w_recv.at[pl.ds(0, G - 1)])
    total = w_recv[0] + w_recv[1] + w_recv[2] + w_recv[3]
    d_all[group] = total
    for t in range(4):
        h_send1[pl.ds(t, S, stride=HROWS), :] = total[:, t * 128 : (t + 1) * 128]
    space_send(4, chunk(h_send1), chunk(h_recv1))
    band_send(5, lambda peer: d_all.at[group], lambda mine: d_all.at[mine])
    keep(h_send1, h_recv1, 0, HROWS)

    lane = lax.broadcasted_iota(jnp.int32, (N, PL * QUART), 1)
    first = signed(lax.broadcasted_iota(jnp.int32, (N, PL * QUART), 0))
    plane = jnp.where(lane >= QUART, 1, 0) + jnp.where(lane >= 2 * QUART, 1, 0)
    second = signed(plane + start)
    third = signed(lane - plane * QUART + group * QUART)
    squared = first * first + second * second + third * third
    coulomb = jnp.where(squared > 0, HARTREE / jnp.maximum(squared, 1).astype(F32), 0.0)

    wait(4, 1, h_recv1.at[pl.ds(0, (S - 1) * HROWS)])
    wide = jnp.concatenate([h_recv1[pl.ds(t, S, stride=HROWS), :] for t in range(4)], axis=1)
    tall = jnp.concatenate(
        [wide[:, r * PL * QUART : (r + 1) * PL * QUART] for r in range(PL)], axis=0
    )
    tall = left(cas_rows, coulomb * left(cas_cols, tall))
    wide = jnp.concatenate(
        [tall[r * S : (r + 1) * S] for r in range(PL)]
        + [jnp.zeros((S, HL - PL * PL * QUART), F32)],
        axis=1,
    )
    for t in range(4):
        h_send2[pl.ds(t, S, stride=HROWS), :] = wide[:, t * 128 : (t + 1) * 128]
    space_send(6, chunk(h_send2), chunk(h_recv2))
    keep(h_send2, h_recv2, 0, HROWS)

    def grid_values(ref):
        planes = []
        for r in range(PL):
            values = jnp.concatenate(
                [
                    jnp.concatenate(
                        [
                            ref[g][:, (r * PL + b) * QUART : (r * PL + b + 1) * QUART]
                            for g in range(G)
                        ],
                        axis=1,
                    )
                    for b in range(PL)
                ],
                axis=0,
            )
            planes.append(left(cas_cols, values))
        return right(jnp.concatenate(planes, axis=0), cas_out[...])

    wait(5, 0, d_all.at[pl.ds(0, G - 1)])
    wait(5, 1, d_all.at[pl.ds(0, G - 1)])
    xc_part = jnp.concatenate([doubled(xc_ref[r]) for r in range(PL)], axis=0)
    xc_part = xc_part * grid_values(d_all)
    acc[:, 0:128] = xc_part[:, 0:128]
    acc[:, 128:256] = xc_part[:, 128:256]
    acc_tail = xc_part[:, 256:384]

    wait(6, 1, h_recv2.at[pl.ds(0, (S - 1) * HROWS)])
    h_all[group] = jnp.concatenate(
        [h_recv2[pl.ds(t, S, stride=HROWS), :] for t in range(4)], axis=1
    )
    band_send(7, lambda peer: h_all.at[group], lambda mine: h_all.at[mine])
    wait(7, 0, h_all.at[pl.ds(0, G - 1)])
    wait(7, 1, h_all.at[pl.ds(0, G - 1)])

    potential = grid_values(h_all) + jnp.concatenate([acc[...], acc_tail], axis=1)
    local = jnp.concatenate([doubled(local_ref[r]) for r in range(PL)], axis=0)
    mixed = right(local * fields[...] + potential * packed[...], lane_minus[...])
    result = left_complex(
        b_minus, jnp.concatenate([mixed[r * N : (r + 1) * N] for r in range(PL)], axis=1)
    )
    for b in range(PL):
        for r in range(PL):
            for t in range(3):
                send2[cell_rows(b, r * PL + t), :] = result[
                    b * S : (b + 1) * S, (r * 3 + t) * 128 : (r * 3 + t + 1) * 128
                ]
        space_send(8 + b, part_chunk(send2, b), part_chunk(recv2, b))
        keep(send2, recv2, b * S * CELL, CELL)
    for r in range(PL):
        pot_ref[r] = jnp.concatenate(
            [potential[r * N : (r + 1) * N, t * 128 : t * 128 + TILE] for t in range(3)], axis=1
        )

    energy = energy_ref[0]

    def read_waves(b, columns):
        seen = hot[b * N : (b + 1) * N, columns]
        found = jnp.dot(
            table[...], jnp.concatenate([seen, seen], axis=0), preferred_element_type=F32
        )
        mask = lax.broadcasted_iota(jnp.int32, (N, READ), 0) == miller_ref[2:3, columns]
        sums = []
        for half in range(2):
            total = None
            for t in range(3):
                at = t * 128 + half * TILE
                kept = jnp.where(
                    mask[t * TILE : (t + 1) * TILE], found[at : at + TILE], 0.0
                )
                total = kept if total is None else total + kept
            sums.append(jnp.sum(total, axis=0, keepdims=True))
        if b > 0:
            sums = [sums[half] + lifted[group, half : half + 1, columns] for half in range(2)]
        if b == PL - 1:
            first = signed(miller_ref[0:1, columns])
            second = signed(miller_ref[1:2, columns])
            third = signed(miller_ref[2:3, columns])
            squared = first * first + second * second + third * third
            diagonal = KINETIC * squared.astype(F32) / float(N * N) - energy
            sums = [sums[half] + diagonal * now_ref[half, 0:1, columns] for half in range(2)]
        for half in range(2):
            lifted[group, half : half + 1, columns] = sums[half]

    blocks = WAVES // BLOCK
    per_block = BLOCK // READ

    def block(ref, at, n):
        return ref.at[at, :, pl.ds(n * BLOCK, BLOCK)]

    for b in range(PL):
        wait(8 + b, 1, recv2.at[every_chunk])
        values = jnp.concatenate(
            [
                jnp.concatenate([recv2[cell_rows(b, r * PL + t), :] for t in range(3)], axis=1)
                for r in range(PL)
            ],
            axis=0,
        )
        result = left_complex(a_minus, values)
        high = result.astype(BF16).astype(F32)
        table[...] = jnp.transpose(jnp.concatenate([high, result - high], axis=0)).astype(BF16)

        def one(step, carry):
            read_waves(b, columns_at(step, READ))
            return carry

        for n in range(blocks):
            lax.fori_loop(n * per_block, (n + 1) * per_block, one, 0)
            if b == PL - 1:
                band_send(
                    11 + n,
                    lambda peer: block(lifted, group, n),
                    lambda mine: block(lifted, mine, n),
                )

    def columns_of_tile(step):
        return pl.ds(pl.multiple_of(step * 128, 128), 128)

    def overlap(step, sums):
        columns = columns_of_tile(step)
        occ_re = occ_ref[0, :, columns]
        occ_im = occ_ref[1, :, columns]
        out = []
        for v in range(G):
            re = lifted[v, 0:1, columns]
            im = lifted[v, 1:2, columns]
            out.append(sums[2 * v] + (occ_re * re + occ_im * im))
            out.append(sums[2 * v + 1] + (occ_re * im - occ_im * re))
        return tuple(out)

    def three(ref, n):
        return ref.at[pl.ds(0, G - 1), :, pl.ds(n * BLOCK, BLOCK)]

    tiles = BLOCK // 128
    sums = tuple(jnp.zeros((16, 128), F32) for _ in range(2 * G))
    for n in range(blocks):
        wait(11 + n, 0, three(lifted, n))
        wait(11 + n, 1, three(lifted, n))
        sums = lax.fori_loop(n * tiles, (n + 1) * tiles, overlap, sums)
    lane = lax.broadcasted_iota(jnp.int32, (16, 128), 1)
    band_of = lane // 16
    own_row = (lane % 16) == lax.broadcasted_iota(jnp.int32, (16, 128), 0)
    matrix = jnp.zeros((16, 128), F32)
    for row in range(2 * G):
        column = jnp.sum(sums[row], axis=1, keepdims=True)
        matrix = jnp.where(band_of == row, column, matrix)
    over_send[0] = jnp.sum(jnp.where(own_row, matrix, 0.0), axis=0, keepdims=True)
    space_send(15, lambda peer: over_send.at[0], lambda mine: over_recv.at[mine])
    over_recv[me] = over_send[0]
    wait(15, 1, over_recv.at[pl.ds(0, S - 1)])
    row_sum = jnp.sum(over_recv[...], axis=0)
    spread = jnp.where(own_row, jnp.broadcast_to(row_sum, (16, 128)), 0.0)
    weights = []
    for row in range(2 * G):
        column = jnp.sum(jnp.where(band_of == row, spread, 0.0), axis=1, keepdims=True)
        weights.append(jnp.broadcast_to(column, (16, 128)))

    def correct(step, carry):
        columns = columns_of_tile(step)
        occ_re = occ_ref[0, :, columns]
        occ_im = occ_ref[1, :, columns]
        for v in range(G):
            w_re, w_im = weights[2 * v], weights[2 * v + 1]
            corr[v, 0:1, columns] = jnp.sum(occ_re * w_re - occ_im * w_im, axis=0, keepdims=True)
            corr[v, 1:2, columns] = jnp.sum(occ_re * w_im + occ_im * w_re, axis=0, keepdims=True)
        return carry

    for n in range(blocks):
        lax.fori_loop(n * tiles, (n + 1) * tiles, correct, 0)
        band_send(
            16 + n, lambda peer: block(corr, peer, n), lambda mine: block(corr_recv, mine, n)
        )

    corr_recv[group] = corr[group]
    beta_old = beta_ref[0]
    partial = [jnp.zeros((1, 1), F32) for _ in range(4)]
    for n in range(blocks):
        wait(16 + n, 1, three(corr_recv, n))
        columns = pl.ds(n * BLOCK, BLOCK)
        for part in range(2):
            removed = (
                corr_recv[0, part : part + 1, columns]
                + corr_recv[1, part : part + 1, columns]
                + corr_recv[2, part : part + 1, columns]
                + corr_recv[3, part : part + 1, columns]
            )
            q = now_ref[part, 0:1, columns]
            p = prev_ref[part, 0:1, columns]
            u = lifted[group, part : part + 1, columns] - removed - beta_old * p
            rest_ref[part, 0:1, columns] = u
            for slot, product in enumerate((u * u, q * u, q * p, q * q)):
                partial[slot] = partial[slot] + jnp.sum(product, axis=1, keepdims=True)
    lane = lax.broadcasted_iota(jnp.int32, (1, 128), 1)
    row = jnp.zeros((1, 128), F32)
    for slot in range(4):
        row = jnp.where(lane == slot, partial[slot], row)
    sum_send1[0] = row
    band_send(20, lambda peer: sum_send1.at[0], lambda mine: sum_recv1.at[mine])
    sum_recv1[group] = sum_send1[0]
    wait(20, 1, sum_recv1.at[pl.ds(0, G - 1)])
    sum_send2[0] = jnp.sum(sum_recv1[...], axis=0)
    space_send(21, lambda peer: sum_send2.at[0], lambda mine: sum_recv2.at[mine])
    sum_recv2[me] = sum_send2[0]

    for part in range(3):
        wait(part, 0, send1.at[every_chunk])
        wait(8 + part, 0, send2.at[every_chunk])
    wait(3, 0, w_send.at[pl.ds(0, G - 1)])
    wait(4, 0, h_send1.at[pl.ds(0, (S - 1) * HROWS)])
    wait(6, 0, h_send2.at[pl.ds(0, (S - 1) * HROWS)])
    wait(15, 0, over_recv.at[pl.ds(0, S - 1)])
    for n in range(blocks):
        wait(16 + n, 0, three(corr, n))
    wait(20, 0, sum_recv1.at[pl.ds(0, G - 1)])

    wait(21, 0, sum_recv2.at[pl.ds(0, S - 1)])
    wait(21, 1, sum_recv2.at[pl.ds(0, S - 1)])
    row = jnp.sum(sum_recv2[...], axis=0)

    def pick(slot):
        return jnp.sum(jnp.where(lane == slot, row, 0.0), axis=1, keepdims=True)

    norm_u, q_u, q_p, norm_q = [pick(slot) for slot in range(4)]
    alpha = (q_u + beta_old * q_p) / ENTRIES
    square = norm_u - 2.0 * alpha * q_u + alpha * alpha * norm_q
    beta_new = jnp.sqrt(square / ENTRIES)
    scalars_ref[...] = jnp.where(lane == 0, alpha, beta_new)


def finish(rest_ref, now_ref, scalars_ref, pot_in, next_ref, coef_ref, pot_ref):
    alpha = scalars_ref[0:1, 0:1]
    beta_new = scalars_ref[0:1, 1:2]
    inverse = 1.0 / beta_new
    for part in range(2):
        next_ref[part] = (rest_ref[part] - alpha * now_ref[part]) * inverse
    coef_ref[...] = scalars_ref[0:1, 0:2]
    pot_ref[...] = pot_in[...]


def per_device(
    lanczos_now,
    lanczos_prev,
    beta_prev,
    orbitals,
    band_energy,
    occupied,
    local_pot,
    xc_kernel,
    miller,
):
    later = [lanczos_prev, orbitals, occupied, local_pot, xc_kernel]
    later += [jnp.asarray(table) for table in make_tables()]
    vmem = pl.BlockSpec(memory_space=pltpu.VMEM)
    smem = pl.BlockSpec(memory_space=pltpu.SMEM)
    anywhere = pl.BlockSpec(memory_space=pl.ANY)
    wide = pltpu.VMEM((3 * S * CELL, 128), F32)
    narrow = pltpu.VMEM((S * HROWS, 128), F32)
    quarter = pltpu.VMEM((G, S, HL), F32)
    band_waves = pltpu.VMEM((G, 2, WAVES), F32)
    real_grid = jax.ShapeDtypeStruct((PL, N, N), F32)
    waves = jax.ShapeDtypeStruct((2, 1, WAVES), F32)
    rest, scalars, potential = pl.pallas_call(
        body,
        out_shape=(waves, jax.ShapeDtypeStruct((1, 128), F32), real_grid),
        in_specs=[vmem, vmem, smem, smem] + [anywhere] * len(later),
        out_specs=(vmem, vmem, vmem),
        scratch_shapes=[pltpu.VMEM(array.shape, array.dtype) for array in later]
        + [
            pltpu.VMEM((PL * N, WAVES), BF16),
            pltpu.VMEM((PL * N, 256), F32),
            wide,
            wide,
            pltpu.VMEM((PL * N, 384), F32),
            pltpu.VMEM((PL * N, 384), F32),
            quarter,
            quarter,
            quarter,
            quarter,
            narrow,
            narrow,
            narrow,
            narrow,
            wide,
            wide,
            pltpu.VMEM((384, 2 * N), BF16),
            band_waves,
            pltpu.VMEM((1, 1, 128), F32),
            pltpu.VMEM((S, 1, 128), F32),
            band_waves,
            band_waves,
            pltpu.VMEM((1, 1, 128), F32),
            pltpu.VMEM((G, 1, 128), F32),
            pltpu.VMEM((1, 1, 128), F32),
            pltpu.VMEM((S, 1, 128), F32),
            pltpu.SemaphoreType.DMA((22, 2)),
            pltpu.SemaphoreType.DMA((len(later),)),
        ],
        compiler_params=pltpu.CompilerParams(
            collective_id=0, has_side_effects=True, vmem_limit_bytes=60 * 1024 * 1024
        ),
    )(lanczos_now, miller, beta_prev, band_energy, *later)
    return pl.pallas_call(
        finish,
        out_shape=(waves, jax.ShapeDtypeStruct((1, 2), F32), real_grid),
        in_specs=[vmem] * 4,
        out_specs=(vmem,) * 3,
    )(rest, lanczos_now, scalars, potential)


def solution(mesh):
    return jax.shard_map(
        per_device,
        mesh=mesh,
        in_specs=(
            P(None, "band", "space"),
            P(None, "band", "space"),
            P(),
            P(None, "band", "space", None, None),
            P("band"),
            P(None, "band", "space"),
            P("space", None, None),
            P("space", None, None),
            P(None, "space"),
        ),
        out_specs=(P(None, "band", "space"), P(), P("space", None, None)),
        check_vma=False,
    )
```

time: 1060 us -> 159 us (0.15)
  local copies, waits for them, and re-layouts: 368 us -> 0 us
  blocking collectives: 300 us -> 0 us
  waiting for transfers between devices: 199 us -> 0 us
  Pallas kernels: 0 us -> 157 us
  matrix products: 97.3 us -> 0 us
  starting transfers between devices: 64 us -> 0 us
  between operations: 17.6 us -> 1.93 us
    psum x3 -> x0, blocking collectives: 281 us -> none  [the longest x1 130 us: per_device(): over_re, over_im = lax.psum((over_re, over_im), 'space')]
    gather x2 -> x0, local copies, waits for them, and re-layouts: 181 us -> none  [the longest x1 90.5 us: per_device(): wave_im = part_im.reshape(count_rows, flat_size)[:, position]]
    pallas_call x0 -> x2, Pallas kernels: none -> 157 us  [the longest x1 155 us: per_device(): pl.pallas_call(body, out_shape=(waves, jax.ShapeDtypeStruct((1, 128), F32...]
    scatter x2 -> x0, local copies, waits for them, and re-layouts: 122 us -> none  [place(): jnp.zeros((band_dev, flat_size), jnp.float32).at[:, position].set(values)]
    all_to_all x8 -> x0, waiting for transfers between devices: 116 us -> none  [the longest x1 18.5 us: per_device(): lax.all_to_all(imag_part, 'space', split_axis=0, concat_axis=1, tiled=True)]
    dot_general x46 -> x0, matrix products: 97.3 us -> none  [the longest x44 87.8 us: along_dim(): product = jnp.dot(shifted, matrix, precision=HIGH)]
    all_to_all x8 -> x0, starting transfers between devices: 64 us -> none  [the longest x1 13.7 us: per_device(): lax.all_to_all(real_part, 'space', split_axis=1, concat_axis=2, tiled=True)]
    psum x1 -> x0, waiting for transfers between devices: 43.2 us -> none  [per_device(): density = lax.psum(partial_value, 'band')]
  transfers between devices with their start and end apart: 10 -> 0, of which waited for: 10 -> 0; matrix products, arithmetic and copies ran while one was open for 4% -> 0% of each run, Pallas kernels for 0% -> 0%
where the time goes in v1:
time: 159 us
  Pallas kernels  157 us (99%)
  between operations  1.93 us (1%)
    pallas_call x1, Pallas kernels, per_device(): pl.pallas_call(body, out_shape=(waves, jax.ShapeDtypeStruct((1, 128), F32...  155 us

profile of v1, /device:TPU:1, one launch (start us, length us, event | category | flops | bytes accessed | tf_op | source)
XLA Modules:
  0.0 159.0 jit_solution(15610895321370156348)
XLA Ops:
  1.9 154.9 %shard_map.202 = (f32[2,1,16384]{2,1,0:T(1,128)}, f32[1,128]{1,0:T(1,128)}, f32[3,192,192]{2,1,0:T(8,128)}) custom-call(f32[2,1,16384]{2,1,0:T(1,128)} %now_ref.1, s32[3,16384]{1,0:T(4,128)} %refs_1_.1, f32[1]{0:T(128)S(6)} %copy.22.refs_2_, f32[1]{0:T(128)S(6)} %copy.23.refs_3_, f32[2,1,16384]{2,1,0:T(1,128)} %refs_4_.1, f32[2,1,3,192,192]{4,3,2,1,0:T(8,128)} %refs_5_.1, ...), custom_call_target="tpu_custom_call" | custom-call | tf_op jit(solution)/shard_map/pallas_call | solution.py:643
  156.9 2.1 %shard_map.203 = (f32[2,1,16384]{2,1,0:T(1,128)}, f32[1,2]{1,0:T(1,128)}, f32[3,192,192]{2,1,0:T(8,128)}) custom-call(f32[2,1,16384]{2,1,0:T(1,128)} %get-tuple-element.6.rest_ref, f32[2,1,16384]{2,1,0:T(1,128)} %now_ref.1, f32[1,128]{1,0:T(1,128)} %get-tuple-element.7.scalars_ref, f32[3,192,192]{2,1,0:T(8,128)} %get-tuple-element.8.pot_in), custom_call_target="tpu_custom_call" | custom-call | tf_op jit(solution)/shard_map/pallas_call | solution.py:683

commit v2 on v1

--- a/solution.py
+++ b/solution.py
@@ -134,10 +134,10 @@
 
 
 def body(*refs):
-    now_ref, miller_ref, beta_ref, energy_ref = refs[:4]
-    later = refs[4:19]
+    now_ref, miller_ref = refs[:2]
+    later = refs[2:19]
     rest_ref, scalars_ref, pot_ref = refs[19:22]
-    held = refs[22:37]
+    held = refs[22:39]
     (
         prev_ref,
         orbit_ref,
@@ -154,6 +154,8 @@
         cas_out,
         cas_rows,
         cas_cols,
+        beta_ref,
+        energy_ref,
     ) = held
     (
         hot,
@@ -162,6 +164,7 @@
         recv1,
         fields,
         packed,
+        xc_part,
         w_send,
         w_recv,
         d_all,
@@ -184,7 +187,7 @@
         sum_recv2,
         sems,
         load_sems,
-    ) = refs[37:]
+    ) = refs[39:]
     me = lax.axis_index("space")
     group = lax.axis_index("band")
     start = me * PL
@@ -197,35 +200,36 @@
 
     barrier = pltpu.get_barrier_semaphore()
 
-    def greet(step, carry):
-        pl.semaphore_signal(
-            barrier, inc=1, device_id={"space": lax.rem(me + step, S)}, device_id_type=MESH
-        )
+    def greet(turn, carry):
+        for step in range(7):
+            peer = lax.rem(me + (turn * 7 + step + 1) * STRIDE, S)
+            pl.semaphore_signal(barrier, inc=1, device_id={"space": peer}, device_id_type=MESH)
         return carry
 
-    lax.fori_loop(1, S, greet, 0)
+    lax.fori_loop(0, (S - 1) // 7, greet, 0)
     for step in range(1, G):
         pl.semaphore_signal(
             barrier, inc=1, device_id={"band": lax.rem(group + step, G)}, device_id_type=MESH
         )
 
     def space_send(phase, source, target):
-        def one(step, carry):
-            peer = lax.rem(me + step * STRIDE, S)
-            pltpu.make_async_remote_copy(
-                src_ref=source(peer),
-                dst_ref=target(me),
-                send_sem=sems.at[phase, 0],
-                recv_sem=sems.at[phase, 1],
-                device_id={"space": peer},
-                device_id_type=MESH,
-            ).start()
+        def one(turn, carry):
+            for step in range(7):
+                peer = lax.rem(me + (turn * 7 + step + 1) * STRIDE, S)
+                pltpu.make_async_remote_copy(
+                    src_ref=source(peer),
+                    dst_ref=target(me),
+                    send_sem=sems.at[phase, 0],
+                    recv_sem=sems.at[phase, 1],
+                    device_id={"space": peer},
+                    device_id_type=MESH,
+                ).start()
             return carry
 
-        lax.fori_loop(1, S, one, 0)
+        lax.fori_loop(0, (S - 1) // 7, one, 0)
 
     def band_send(phase, source, target):
-        for step in range(1, G):
+        for step in (2, 1, 3):
             peer = lax.rem(group + step, G)
             pltpu.make_async_remote_copy(
                 src_ref=source(peer),
@@ -277,7 +281,7 @@
             return carry
 
         acc[...] = jnp.zeros_like(acc)
-        lax.fori_loop(0, WAVES // PLACE, one, 0)
+        lax.fori_loop(0, WAVES // PLACE, one, 0, unroll=2)
 
     def values_of(columns):
         re_high, re_low = split(now_ref[0, 0:1, columns])
@@ -399,11 +403,10 @@
 
     wait(5, 0, d_all.at[pl.ds(0, G - 1)])
     wait(5, 1, d_all.at[pl.ds(0, G - 1)])
-    xc_part = jnp.concatenate([doubled(xc_ref[r]) for r in range(PL)], axis=0)
-    xc_part = xc_part * grid_values(d_all)
-    acc[:, 0:128] = xc_part[:, 0:128]
-    acc[:, 128:256] = xc_part[:, 128:256]
-    acc_tail = xc_part[:, 256:384]
+    known = grid_values(d_all) * jnp.concatenate([doubled(xc_ref[r]) for r in range(PL)], axis=0)
+    local = jnp.concatenate([doubled(local_ref[r]) for r in range(PL)], axis=0)
+    fields[...] = local * fields[...] + known * packed[...]
+    xc_part[...] = known
 
     wait(6, 1, h_recv2.at[pl.ds(0, (S - 1) * HROWS)])
     h_all[group] = jnp.concatenate(
@@ -413,9 +416,8 @@
     wait(7, 0, h_all.at[pl.ds(0, G - 1)])
     wait(7, 1, h_all.at[pl.ds(0, G - 1)])
 
-    potential = grid_values(h_all) + jnp.concatenate([acc[...], acc_tail], axis=1)
-    local = jnp.concatenate([doubled(local_ref[r]) for r in range(PL)], axis=0)
-    mixed = right(local * fields[...] + potential * packed[...], lane_minus[...])
+    hartree = grid_values(h_all)
+    mixed = right(fields[...] + hartree * packed[...], lane_minus[...])
     result = left_complex(
         b_minus, jnp.concatenate([mixed[r * N : (r + 1) * N] for r in range(PL)], axis=1)
     )
@@ -427,12 +429,13 @@
                 ]
         space_send(8 + b, part_chunk(send2, b), part_chunk(recv2, b))
         keep(send2, recv2, b * S * CELL, CELL)
+    potential = hartree + xc_part[...]
     for r in range(PL):
         pot_ref[r] = jnp.concatenate(
             [potential[r * N : (r + 1) * N, t * 128 : t * 128 + TILE] for t in range(3)], axis=1
         )
 
-    energy = energy_ref[0]
+    energy = energy_ref[0:1].reshape(1, 1)
 
     def read_waves(b, columns):
         seen = hot[b * N : (b + 1) * N, columns]
@@ -486,7 +489,7 @@
             return carry
 
         for n in range(blocks):
-            lax.fori_loop(n * per_block, (n + 1) * per_block, one, 0)
+            lax.fori_loop(n * per_block, (n + 1) * per_block, one, 0, unroll=2)
             if b == PL - 1:
                 band_send(
                     11 + n,
@@ -517,7 +520,7 @@
     for n in range(blocks):
         wait(11 + n, 0, three(lifted, n))
         wait(11 + n, 1, three(lifted, n))
-        sums = lax.fori_loop(n * tiles, (n + 1) * tiles, overlap, sums)
+        sums = lax.fori_loop(n * tiles, (n + 1) * tiles, overlap, sums, unroll=4)
     lane = lax.broadcasted_iota(jnp.int32, (16, 128), 1)
     band_of = lane // 16
     own_row = (lane % 16) == lax.broadcasted_iota(jnp.int32, (16, 128), 0)
@@ -547,13 +550,13 @@
         return carry
 
     for n in range(blocks):
-        lax.fori_loop(n * tiles, (n + 1) * tiles, correct, 0)
+        lax.fori_loop(n * tiles, (n + 1) * tiles, correct, 0, unroll=4)
         band_send(
             16 + n, lambda peer: block(corr, peer, n), lambda mine: block(corr_recv, mine, n)
         )
 
     corr_recv[group] = corr[group]
-    beta_old = beta_ref[0]
+    beta_old = beta_ref[0:1].reshape(1, 1)
     partial = [jnp.zeros((1, 1), F32) for _ in range(4)]
     for n in range(blocks):
         wait(16 + n, 1, three(corr_recv, n))
@@ -608,14 +611,16 @@
     scalars_ref[...] = jnp.where(lane == 0, alpha, beta_new)
 
 
-def finish(rest_ref, now_ref, scalars_ref, pot_in, next_ref, coef_ref, pot_ref):
+def finish(rest_ref, now_ref, scalars_ref, pot_in, next_ref, coef_ref, pot_ref, sem):
+    through = pltpu.make_async_copy(pot_in, pot_ref, sem)
+    through.start()
     alpha = scalars_ref[0:1, 0:1]
     beta_new = scalars_ref[0:1, 1:2]
     inverse = 1.0 / beta_new
     for part in range(2):
         next_ref[part] = (rest_ref[part] - alpha * now_ref[part]) * inverse
     coef_ref[...] = scalars_ref[0:1, 0:2]
-    pot_ref[...] = pot_in[...]
+    through.wait()
 
 
 def per_device(
@@ -631,9 +636,9 @@
 ):
     later = [lanczos_prev, orbitals, occupied, local_pot, xc_kernel]
     later += [jnp.asarray(table) for table in make_tables()]
+    later += [beta_prev, band_energy]
     vmem = pl.BlockSpec(memory_space=pltpu.VMEM)
-    smem = pl.BlockSpec(memory_space=pltpu.SMEM)
-    anywhere = pl.BlockSpec(memory_space=pl.ANY)
+    in_hbm = pl.BlockSpec(memory_space=pltpu.HBM)
     wide = pltpu.VMEM((3 * S * CELL, 128), F32)
     narrow = pltpu.VMEM((S * HROWS, 128), F32)
     quarter = pltpu.VMEM((G, S, HL), F32)
@@ -643,7 +648,7 @@
     rest, scalars, potential = pl.pallas_call(
         body,
         out_shape=(waves, jax.ShapeDtypeStruct((1, 128), F32), real_grid),
-        in_specs=[vmem, vmem, smem, smem] + [anywhere] * len(later),
+        in_specs=[vmem, vmem] + [in_hbm] * len(later),
         out_specs=(vmem, vmem, vmem),
         scratch_shapes=[pltpu.VMEM(array.shape, array.dtype) for array in later]
         + [
@@ -651,6 +656,7 @@
             pltpu.VMEM((PL * N, 256), F32),
             wide,
             wide,
+            pltpu.VMEM((PL * N, 384), F32),
             pltpu.VMEM((PL * N, 384), F32),
             pltpu.VMEM((PL * N, 384), F32),
             quarter,
@@ -679,12 +685,13 @@
         compiler_params=pltpu.CompilerParams(
             collective_id=0, has_side_effects=True, vmem_limit_bytes=60 * 1024 * 1024
         ),
-    )(lanczos_now, miller, beta_prev, band_energy, *later)
+    )(lanczos_now, miller, *later)
     return pl.pallas_call(
         finish,
         out_shape=(waves, jax.ShapeDtypeStruct((1, 2), F32), real_grid),
-        in_specs=[vmem] * 4,
-        out_specs=(vmem,) * 3,
+        in_specs=[vmem, vmem, vmem, in_hbm],
+        out_specs=(vmem, vmem, in_hbm),
+        scratch_shapes=[pltpu.SemaphoreType.DMA],
     )(rest, lanczos_now, scalars, potential)
 
 

time: 159 us -> 171 us (1.075)
  Pallas kernels: 157 us -> 168 us
    pallas_call x1, Pallas kernels: 2.1 us -> 20.6 us  [per_device(): pl.pallas_call(finish, out_shape=(waves, jax.ShapeDtypeStruct((1, 2), F32...]
    pallas_call x1, Pallas kernels: 155 us -> 148 us  [per_device(): pl.pallas_call(body, out_shape=(waves, jax.ShapeDtypeStruct((1, 128), F32...]
where the time goes in v2:
time: 171 us
  Pallas kernels  168 us (98%)
  between operations  2.11 us (1%)
    pallas_call x1, Pallas kernels, per_device(): pl.pallas_call(body, out_shape=(waves, jax.ShapeDtypeStruct((1, 128), F32...  148 us
    pallas_call x1, Pallas kernels, per_device(): pl.pallas_call(finish, out_shape=(waves, jax.ShapeDtypeStruct((1, 2), F32...  20.6 us

profile of v2, /device:TPU:1, one launch (start us, length us, event | category | flops | bytes accessed | tf_op | source)
XLA Modules:
  0.0 170.6 jit_solution(3441603378114289706)
XLA Ops:
  1.9 147.9 %shard_map.202 = (f32[2,1,16384]{2,1,0:T(1,128)}, f32[1,128]{1,0:T(1,128)}, f32[3,192,192]{2,1,0:T(8,128)}) custom-call(f32[2,1,16384]{2,1,0:T(1,128)} %now_ref.1, s32[3,16384]{1,0:T(4,128)} %refs_1_.1, f32[2,1,16384]{2,1,0:T(1,128)} %refs_2_.1, f32[2,1,3,192,192]{4,3,2,1,0:T(8,128)} %refs_3_.1, f32[2,16,16384]{2,1,0:T(8,128)} %refs_4_.1, ...), custom_call_target="tpu_custom_call" | custom-call | tf_op jit(solution)/shard_map/pallas_call | solution.py:648
  149.8 20.6 %shard_map.203 = (f32[2,1,16384]{2,1,0:T(1,128)}, f32[1,2]{1,0:T(1,128)}, f32[3,192,192]{2,1,0:T(8,128)}) custom-call(f32[2,1,16384]{2,1,0:T(1,128)} %get-tuple-element.6.rest_ref, f32[2,1,16384]{2,1,0:T(1,128)} %now_ref.1, f32[1,128]{1,0:T(1,128)} %get-tuple-element.7.scalars_ref, f32[3,192,192]{2,1,0:T(8,128)} %get-tuple-element.8.pot_in), custom_call_target="tpu_custom_call" | custom-call | tf_op jit(solution)/shard_map/pallas_call | solution.py:689

commit v3 on v2

--- a/solution.py
+++ b/solution.py
@@ -39,7 +39,7 @@
 
 def left_table(table):
     high, low = split_np(table)
-    return np.concatenate([high, high, low], axis=1)
+    return np.concatenate([high, low], axis=0)
 
 
 def right_table(table):
@@ -69,7 +69,7 @@
             cosine[row_order][:, column_order],
             sign * sine[row_order][:, column_order],
         ]
-        return left_table(np.concatenate(both, axis=1))
+        return left_table(np.concatenate(both, axis=0))
 
     cas = cosine + sine
     cas_in = np.zeros((2 * N, N))
@@ -98,8 +98,10 @@
 
 def left(table_ref, values):
     high, low = split(values)
-    stacked = jnp.concatenate([high, low, high], axis=0)
-    return jnp.dot(table_ref[...], stacked, preferred_element_type=F32)
+    rows = table_ref.shape[0] // 2
+    by_high = jnp.dot(table_ref[...], high, preferred_element_type=F32)
+    by_low = jnp.dot(table_ref[0:rows], low, preferred_element_type=F32)
+    return by_high[0:rows] + (by_high[rows:] + by_low)
 
 
 def right(values, table):
@@ -118,7 +120,8 @@
 
 
 def left_complex(table_ref, values):
-    return left(table_ref, jnp.concatenate([values, times_i(values)], axis=0))
+    both = left(table_ref, values)
+    return both[0:N] + times_i(both[N:])
 
 
 def signed(indices):
@@ -439,9 +442,7 @@
 
     def read_waves(b, columns):
         seen = hot[b * N : (b + 1) * N, columns]
-        found = jnp.dot(
-            table[...], jnp.concatenate([seen, seen], axis=0), preferred_element_type=F32
-        )
+        found = jnp.dot(table[...], seen, preferred_element_type=F32)
         mask = lax.broadcasted_iota(jnp.int32, (N, READ), 0) == miller_ref[2:3, columns]
         sums = []
         for half in range(2):
@@ -449,7 +450,9 @@
             for t in range(3):
                 at = t * 128 + half * TILE
                 kept = jnp.where(
-                    mask[t * TILE : (t + 1) * TILE], found[at : at + TILE], 0.0
+                    mask[t * TILE : (t + 1) * TILE],
+                    found[at : at + TILE] + found[384 + at : 384 + at + TILE],
+                    0.0,
                 )
                 total = kept if total is None else total + kept
             sums.append(jnp.sum(total, axis=0, keepdims=True))
@@ -482,7 +485,7 @@
         )
         result = left_complex(a_minus, values)
         high = result.astype(BF16).astype(F32)
-        table[...] = jnp.transpose(jnp.concatenate([high, result - high], axis=0)).astype(BF16)
+        table[...] = jnp.transpose(jnp.concatenate([high, result - high], axis=1)).astype(BF16)
 
         def one(step, carry):
             read_waves(b, columns_at(step, READ))
@@ -611,16 +614,14 @@
     scalars_ref[...] = jnp.where(lane == 0, alpha, beta_new)
 
 
-def finish(rest_ref, now_ref, scalars_ref, pot_in, next_ref, coef_ref, pot_ref, sem):
-    through = pltpu.make_async_copy(pot_in, pot_ref, sem)
-    through.start()
+def finish(rest_ref, now_ref, scalars_ref, pot_in, next_ref, coef_ref, pot_ref):
     alpha = scalars_ref[0:1, 0:1]
     beta_new = scalars_ref[0:1, 1:2]
     inverse = 1.0 / beta_new
     for part in range(2):
         next_ref[part] = (rest_ref[part] - alpha * now_ref[part]) * inverse
     coef_ref[...] = scalars_ref[0:1, 0:2]
-    through.wait()
+    pot_ref[...] = pot_in[...]
 
 
 def per_device(
@@ -669,7 +670,7 @@
             narrow,
             wide,
             wide,
-            pltpu.VMEM((384, 2 * N), BF16),
+            pltpu.VMEM((768, N), BF16),
             band_waves,
             pltpu.VMEM((1, 1, 128), F32),
             pltpu.VMEM((S, 1, 128), F32),
@@ -689,9 +690,8 @@
     return pl.pallas_call(
         finish,
         out_shape=(waves, jax.ShapeDtypeStruct((1, 2), F32), real_grid),
-        in_specs=[vmem, vmem, vmem, in_hbm],
-        out_specs=(vmem, vmem, in_hbm),
-        scratch_shapes=[pltpu.SemaphoreType.DMA],
+        in_specs=[vmem] * 4,
+        out_specs=(vmem,) * 3,
     )(rest, lanczos_now, scalars, potential)
 
 

time: 171 us -> 153 us (0.89)
  Pallas kernels: 168 us -> 151 us
    pallas_call x1, Pallas kernels: 20.6 us -> 2.1 us  [per_device(): pl.pallas_call(finish, out_shape=(waves, jax.ShapeDtypeStruct((1, 2), F32...]
where the time goes in v3:
time: 153 us
  Pallas kernels  151 us (99%)
  between operations  1.93 us (1%)
    pallas_call x1, Pallas kernels, per_device(): pl.pallas_call(body, out_shape=(waves, jax.ShapeDtypeStruct((1, 128), F32...  149 us

profile of v3, /device:TPU:1, one launch (start us, length us, event | category | flops | bytes accessed | tf_op | source)
XLA Modules:
  0.0 152.9 jit_solution(13123311526727807353)
XLA Ops:
  1.9 148.9 %shard_map.202 = (f32[2,1,16384]{2,1,0:T(1,128)}, f32[1,128]{1,0:T(1,128)}, f32[3,192,192]{2,1,0:T(8,128)}) custom-call(f32[2,1,16384]{2,1,0:T(1,128)} %now_ref.1, s32[3,16384]{1,0:T(4,128)} %refs_1_.1, f32[2,1,16384]{2,1,0:T(1,128)} %refs_2_.1, f32[2,1,3,192,192]{4,3,2,1,0:T(8,128)} %refs_3_.1, f32[2,16,16384]{2,1,0:T(8,128)} %refs_4_.1, ...), custom_call_target="tpu_custom_call" | custom-call | tf_op jit(solution)/shard_map/pallas_call | solution.py:649
  150.8 2.1 %shard_map.203 = (f32[2,1,16384]{2,1,0:T(1,128)}, f32[1,2]{1,0:T(1,128)}, f32[3,192,192]{2,1,0:T(8,128)}) custom-call(f32[2,1,16384]{2,1,0:T(1,128)} %get-tuple-element.6.rest_ref, f32[2,1,16384]{2,1,0:T(1,128)} %now_ref.1, f32[1,128]{1,0:T(1,128)} %get-tuple-element.7.scalars_ref, f32[3,192,192]{2,1,0:T(8,128)} %get-tuple-element.8.pot_in), custom_call_target="tpu_custom_call" | custom-call | tf_op jit(solution)/shard_map/pallas_call | solution.py:690

commit v4 on v3

--- a/solution.py
+++ b/solution.py
@@ -16,6 +16,8 @@
 HARTREE = 4.0
 N = 192
 S = 64
+Z = 8
+C = 8
 G = 4
 PL = 3
 CELL = 9
@@ -164,6 +166,7 @@
         hot,
         acc,
         send1,
+        turn1,
         recv1,
         fields,
         packed,
@@ -177,6 +180,7 @@
         h_send2,
         h_recv2,
         send2,
+        turn2,
         recv2,
         table,
         lifted,
@@ -246,8 +250,44 @@
     def wait(phase, side, region):
         pltpu.make_async_copy(region, region, sems.at[phase, side]).wait()
 
-    def part_chunk(ref, part):
-        return lambda at: ref.at[pl.ds(part * S * CELL + at * CELL, CELL)]
+    here_z = me // C
+    here_c = lax.rem(me, C)
+    every_step = pl.ds(0, (Z - 1) * C * CELL)
+
+    def z_send(phase, part, source, target):
+        def rows(z):
+            return pl.ds(part * S * CELL + z * (C * CELL), C * CELL)
+
+        for step in (4, 3, 5, 2, 6, 1, 7):
+            z = lax.rem(here_z + step, Z)
+            pltpu.make_async_remote_copy(
+                src_ref=source.at[rows(z)],
+                dst_ref=target.at[rows(here_z)],
+                send_sem=sems.at[phase, 0],
+                recv_sem=sems.at[phase, 1],
+                device_id={"space": z * C + here_c},
+                device_id_type=MESH,
+            ).start()
+        own = pl.ds(pl.multiple_of(part * S * CELL + here_z * (C * CELL), 8), C * CELL)
+        target[own, :] = source[own, :]
+
+    def c_send(z_phase, phase, part, source, target):
+        wait(z_phase, 1, source.at[every_step])
+        source_view = source.reshape(3 * Z, C * CELL, 128)
+        target_view = target.reshape(3 * Z, C * CELL, 128)
+        for step in (4, 3, 5, 2, 6, 1, 7):
+            c = lax.rem(here_c + step, C)
+            pltpu.make_async_remote_copy(
+                src_ref=source_view.at[pl.ds(part * Z, Z), pl.ds(c * CELL, CELL)],
+                dst_ref=target_view.at[pl.ds(part * Z, Z), pl.ds(here_c * CELL, CELL)],
+                send_sem=sems.at[phase, 0],
+                recv_sem=sems.at[phase, 1],
+                device_id={"space": here_z * C + c},
+                device_id_type=MESH,
+            ).start()
+        for z in range(Z):
+            own = pl.ds(part * S * CELL + z * (C * CELL) + here_c * CELL, CELL)
+            target[own, :] = source[own, :]
 
     def chunk(ref):
         return lambda at: ref.at[pl.ds(at * HROWS, HROWS)]
@@ -306,8 +346,10 @@
                 ]
         if t == 0:
             pl.semaphore_wait(barrier, S - 1 + G - 1)
-        space_send(t, part_chunk(send1, t), part_chunk(recv1, t))
-        keep(send1, recv1, t * S * CELL, CELL)
+        z_send(22 + t, t, send1, turn1)
+        if t > 0:
+            c_send(22 + t - 1, t - 1, t - 1, turn1, recv1)
+    c_send(24, 2, 2, turn1, recv1)
 
     for at in range(len(later)):
         if at != 7:
@@ -321,9 +363,8 @@
             pieces += [re[:, t * TILE : (t + 1) * TILE], im[:, t * TILE : (t + 1) * TILE]]
         packed[r * N : (r + 1) * N] = jnp.concatenate(pieces, axis=1)
 
-    every_chunk = pl.ds(0, (S - 1) * CELL)
     for t in range(3):
-        wait(t, 1, recv1.at[every_chunk])
+        wait(t, 1, recv1.at[every_step])
         values = jnp.concatenate(
             [
                 jnp.concatenate([recv1[cell_rows(t, r * PL + b), :] for r in range(PL)], axis=1)
@@ -430,8 +471,7 @@
                 send2[cell_rows(b, r * PL + t), :] = result[
                     b * S : (b + 1) * S, (r * 3 + t) * 128 : (r * 3 + t + 1) * 128
                 ]
-        space_send(8 + b, part_chunk(send2, b), part_chunk(recv2, b))
-        keep(send2, recv2, b * S * CELL, CELL)
+        z_send(25 + b, b, send2, turn2)
     potential = hartree + xc_part[...]
     for r in range(PL):
         pot_ref[r] = jnp.concatenate(
@@ -474,8 +514,9 @@
     def block(ref, at, n):
         return ref.at[at, :, pl.ds(n * BLOCK, BLOCK)]
 
+    c_send(25, 8, 0, turn2, recv2)
     for b in range(PL):
-        wait(8 + b, 1, recv2.at[every_chunk])
+        wait(8 + b, 1, recv2.at[every_step])
         values = jnp.concatenate(
             [
                 jnp.concatenate([recv2[cell_rows(b, r * PL + t), :] for t in range(3)], axis=1)
@@ -493,6 +534,8 @@
 
         for n in range(blocks):
             lax.fori_loop(n * per_block, (n + 1) * per_block, one, 0, unroll=2)
+            if n == 1 and b < PL - 1:
+                c_send(25 + b + 1, 8 + b + 1, b + 1, turn2, recv2)
             if b == PL - 1:
                 band_send(
                     11 + n,
@@ -590,8 +633,8 @@
     sum_recv2[me] = sum_send2[0]
 
     for part in range(3):
-        wait(part, 0, send1.at[every_chunk])
-        wait(8 + part, 0, send2.at[every_chunk])
+        for phase in (part, 8 + part, 22 + part, 25 + part):
+            wait(phase, 0, send1.at[every_step])
     wait(3, 0, w_send.at[pl.ds(0, G - 1)])
     wait(4, 0, h_send1.at[pl.ds(0, (S - 1) * HROWS)])
     wait(6, 0, h_send2.at[pl.ds(0, (S - 1) * HROWS)])
@@ -657,6 +700,7 @@
             pltpu.VMEM((PL * N, 256), F32),
             wide,
             wide,
+            wide,
             pltpu.VMEM((PL * N, 384), F32),
             pltpu.VMEM((PL * N, 384), F32),
             pltpu.VMEM((PL * N, 384), F32),
@@ -670,6 +714,7 @@
             narrow,
             wide,
             wide,
+            wide,
             pltpu.VMEM((768, N), BF16),
             band_waves,
             pltpu.VMEM((1, 1, 128), F32),
@@ -680,7 +725,7 @@
             pltpu.VMEM((G, 1, 128), F32),
             pltpu.VMEM((1, 1, 128), F32),
             pltpu.VMEM((S, 1, 128), F32),
-            pltpu.SemaphoreType.DMA((22, 2)),
+            pltpu.SemaphoreType.DMA((28, 2)),
             pltpu.SemaphoreType.DMA((len(later),)),
         ],
         compiler_params=pltpu.CompilerParams(

time: 153 us -> 161 us (1.052)
  Pallas kernels: 151 us -> 159 us
    pallas_call x1, Pallas kernels: 149 us -> 157 us  [per_device(): pl.pallas_call(body, out_shape=(waves, jax.ShapeDtypeStruct((1, 128), F32...]
where the time goes in v4:
time: 161 us
  Pallas kernels  159 us (99%)
  between operations  1.93 us (1%)
    pallas_call x1, Pallas kernels, per_device(): pl.pallas_call(body, out_shape=(waves, jax.ShapeDtypeStruct((1, 128), F32...  157 us

profile of v4, /device:TPU:1, one launch (start us, length us, event | category | flops | bytes accessed | tf_op | source)
XLA Modules:
  0.0 160.9 jit_solution(18407158734464018743)
XLA Ops:
  1.9 156.9 %shard_map.202 = (f32[2,1,16384]{2,1,0:T(1,128)}, f32[1,128]{1,0:T(1,128)}, f32[3,192,192]{2,1,0:T(8,128)}) custom-call(f32[2,1,16384]{2,1,0:T(1,128)} %now_ref.1, s32[3,16384]{1,0:T(4,128)} %refs_1_.1, f32[2,1,16384]{2,1,0:T(1,128)} %refs_2_.1, f32[2,1,3,192,192]{4,3,2,1,0:T(8,128)} %refs_3_.1, f32[2,16,16384]{2,1,0:T(8,128)} %refs_4_.1, ...), custom_call_target="tpu_custom_call" | custom-call | tf_op jit(solution)/shard_map/pallas_call | solution.py:692
  158.8 2.1 %shard_map.203 = (f32[2,1,16384]{2,1,0:T(1,128)}, f32[1,2]{1,0:T(1,128)}, f32[3,192,192]{2,1,0:T(8,128)}) custom-call(f32[2,1,16384]{2,1,0:T(1,128)} %get-tuple-element.6.rest_ref, f32[2,1,16384]{2,1,0:T(1,128)} %now_ref.1, f32[1,128]{1,0:T(1,128)} %get-tuple-element.7.scalars_ref, f32[3,192,192]{2,1,0:T(8,128)} %get-tuple-element.8.pot_in), custom_call_target="tpu_custom_call" | custom-call | tf_op jit(solution)/shard_map/pallas_call | solution.py:735

commit v5 on v3

--- a/solution.py
+++ b/solution.py
@@ -21,12 +21,17 @@
 CELL = 9
 HROWS = 4
 QUART = N // G
+THIRD = PL * QUART
 HL = 512
+LOW = 4
+HIGH = S // LOW
 TILE = 64
 WAVES = 16384
 PLACE = 2048
-READ = 1024
+READ = 256
 BLOCK = 4096
+W_PHASE = (3, 22, 23, 24)
+H_PHASE = (7, 25, 26, 27)
 STRIDE = 29
 ENTRIES = float(2 * G * WAVES * S)
 
@@ -211,9 +216,14 @@
 
     lax.fori_loop(0, (S - 1) // 7, greet, 0)
     for step in range(1, G):
-        pl.semaphore_signal(
-            barrier, inc=1, device_id={"band": lax.rem(group + step, G)}, device_id_type=MESH
-        )
+        for low in range(LOW):
+            peer = me // LOW * LOW + lax.rem(me + low, LOW)
+            pl.semaphore_signal(
+                barrier,
+                inc=1,
+                device_id={"band": lax.rem(group + step, G), "space": peer},
+                device_id_type=MESH,
+            )
 
     def space_send(phase, source, target):
         def one(turn, carry):
@@ -305,7 +315,7 @@
                     r * S : (r + 1) * S, b * 128 : (b + 1) * 128
                 ]
         if t == 0:
-            pl.semaphore_wait(barrier, S - 1 + G - 1)
+            pl.semaphore_wait(barrier, S - 1 + (G - 1) * LOW)
         space_send(t, part_chunk(send1, t), part_chunk(recv1, t))
         keep(send1, recv1, t * S * CELL, CELL)
 
@@ -339,25 +349,45 @@
         else:
             fields[...] += result
 
-    columns_of = right(2.0 * fields[...] * packed[...], cas_in[...])
-    columns_of = [left(cas_rows, columns_of[r * N : (r + 1) * N]) for r in range(PL)]
-
-    for g in range(G):
-        pieces = []
-        for r in range(PL):
-            for b in range(PL):
-                pieces.append(columns_of[r][b * S : (b + 1) * S, g * QUART : (g + 1) * QUART])
-        pieces.append(jnp.zeros((S, HL - PL * PL * QUART), F32))
-        w_send[g] = jnp.concatenate(pieces, axis=1)
-
-    band_send(3, lambda peer: w_send.at[peer], lambda mine: w_recv.at[mine])
+    def tile_at(t):
+        return pl.ds(t * 128, 128)
+
+    tails = [[] for _ in range(G)]
+    for r in range(PL):
+        plane = pl.ds(r * N, N)
+        values = left(cas_rows, right(2.0 * fields[plane, :] * packed[plane, :], cas_in[...]))
+        for g in range(G):
+            row = jnp.concatenate(
+                [
+                    values[b * S : (b + 1) * S, g * QUART : (g + 1) * QUART]
+                    for b in range(PL)
+                ],
+                axis=1,
+            )
+            w_send[g, :, tile_at(r)] = row[:, :128]
+            tails[g].append(row[:, 128:])
+        if r == PL - 1:
+            for g in range(G):
+                w_send[g, :, tile_at(PL)] = jnp.concatenate(
+                    tails[g] + [jnp.zeros((S, HL - PL * THIRD), F32)], axis=1
+                )
+        for t in (r,) if r < PL - 1 else (r, PL):
+            band_send(
+                W_PHASE[t],
+                lambda peer: w_send.at[peer, :, tile_at(t)],
+                lambda mine: w_recv.at[mine, :, tile_at(t)],
+            )
+
     w_recv[group] = w_send[group]
-    wait(3, 1, w_recv.at[pl.ds(0, G - 1)])
-    total = w_recv[0] + w_recv[1] + w_recv[2] + w_recv[3]
+    totals = []
+    for t in range(4):
+        wait(W_PHASE[t], 1, w_recv.at[pl.ds(0, G - 1), :, tile_at(t)])
+        parts = [w_recv[g, :, tile_at(t)] for g in range(G)]
+        totals.append(parts[0] + parts[1] + parts[2] + parts[3])
+        h_send1[pl.ds(t, S, stride=HROWS), :] = totals[t]
+    total = jnp.concatenate(totals, axis=1)
+    space_send(4, chunk(h_send1), chunk(h_recv1))
     d_all[group] = total
-    for t in range(4):
-        h_send1[pl.ds(t, S, stride=HROWS), :] = total[:, t * 128 : (t + 1) * 128]
-    space_send(4, chunk(h_send1), chunk(h_recv1))
     band_send(5, lambda peer: d_all.at[group], lambda mine: d_all.at[mine])
     keep(h_send1, h_recv1, 0, HROWS)
 
@@ -370,60 +400,67 @@
     coulomb = jnp.where(squared > 0, HARTREE / jnp.maximum(squared, 1).astype(F32), 0.0)
 
     wait(4, 1, h_recv1.at[pl.ds(0, (S - 1) * HROWS)])
-    wide = jnp.concatenate([h_recv1[pl.ds(t, S, stride=HROWS), :] for t in range(4)], axis=1)
+    pieces = [h_recv1[pl.ds(t, S, stride=HROWS), :] for t in range(4)]
     tall = jnp.concatenate(
-        [wide[:, r * PL * QUART : (r + 1) * PL * QUART] for r in range(PL)], axis=0
+        [
+            jnp.concatenate([pieces[r], pieces[PL][:, r * 16 : (r + 1) * 16]], axis=1)
+            for r in range(PL)
+        ],
+        axis=0,
     )
     tall = left(cas_rows, coulomb * left(cas_cols, tall))
-    wide = jnp.concatenate(
-        [tall[r * S : (r + 1) * S] for r in range(PL)]
-        + [jnp.zeros((S, HL - PL * PL * QUART), F32)],
+    for r in range(PL):
+        h_send2[pl.ds(r, S, stride=HROWS), :] = tall[r * S : (r + 1) * S, :128]
+    h_send2[pl.ds(PL, S, stride=HROWS), :] = jnp.concatenate(
+        [tall[r * S : (r + 1) * S, 128:] for r in range(PL)]
+        + [jnp.zeros((S, HL - PL * THIRD), F32)],
         axis=1,
     )
-    for t in range(4):
-        h_send2[pl.ds(t, S, stride=HROWS), :] = wide[:, t * 128 : (t + 1) * 128]
     space_send(6, chunk(h_send2), chunk(h_recv2))
     keep(h_send2, h_recv2, 0, HROWS)
 
-    def grid_values(ref):
-        planes = []
-        for r in range(PL):
-            values = jnp.concatenate(
-                [
-                    jnp.concatenate(
-                        [
-                            ref[g][:, (r * PL + b) * QUART : (r * PL + b + 1) * QUART]
-                            for g in range(G)
-                        ],
-                        axis=1,
-                    )
-                    for b in range(PL)
-                ],
-                axis=0,
+    def grid_values(ref, r):
+        rows = [
+            jnp.concatenate(
+                [ref[g, :, tile_at(r)], ref[g, :, tile_at(PL)][:, r * 16 : (r + 1) * 16]], axis=1
             )
-            planes.append(left(cas_cols, values))
-        return right(jnp.concatenate(planes, axis=0), cas_out[...])
+            for g in range(G)
+        ]
+        values = jnp.concatenate(
+            [
+                jnp.concatenate([row[:, b * QUART : (b + 1) * QUART] for row in rows], axis=1)
+                for b in range(PL)
+            ],
+            axis=0,
+        )
+        return right(left(cas_cols, values), cas_out[...])
 
     wait(5, 0, d_all.at[pl.ds(0, G - 1)])
     wait(5, 1, d_all.at[pl.ds(0, G - 1)])
-    known = grid_values(d_all) * jnp.concatenate([doubled(xc_ref[r]) for r in range(PL)], axis=0)
-    local = jnp.concatenate([doubled(local_ref[r]) for r in range(PL)], axis=0)
-    fields[...] = local * fields[...] + known * packed[...]
-    xc_part[...] = known
+    for r in range(PL):
+        plane = pl.ds(r * N, N)
+        known = grid_values(d_all, r) * doubled(xc_ref[r])
+        fields[plane, :] = doubled(local_ref[r]) * fields[plane, :] + known * packed[plane, :]
+        xc_part[plane, :] = known
 
     wait(6, 1, h_recv2.at[pl.ds(0, (S - 1) * HROWS)])
-    h_all[group] = jnp.concatenate(
-        [h_recv2[pl.ds(t, S, stride=HROWS), :] for t in range(4)], axis=1
-    )
-    band_send(7, lambda peer: h_all.at[group], lambda mine: h_all.at[mine])
-    wait(7, 0, h_all.at[pl.ds(0, G - 1)])
-    wait(7, 1, h_all.at[pl.ds(0, G - 1)])
-
-    hartree = grid_values(h_all)
-    mixed = right(fields[...] + hartree * packed[...], lane_minus[...])
-    result = left_complex(
-        b_minus, jnp.concatenate([mixed[r * N : (r + 1) * N] for r in range(PL)], axis=1)
-    )
+    for t in (PL, 0, 1, 2):
+        h_all[group, :, tile_at(t)] = h_recv2[pl.ds(t, S, stride=HROWS), :]
+        band_send(
+            H_PHASE[t],
+            lambda peer: h_all.at[group, :, tile_at(t)],
+            lambda mine: h_all.at[mine, :, tile_at(t)],
+        )
+    mixed = []
+    for r in range(PL):
+        plane = pl.ds(r * N, N)
+        for t in (PL, 0) if r == 0 else (r,):
+            wait(H_PHASE[t], 0, h_all.at[pl.ds(0, G - 1), :, tile_at(t)])
+            wait(H_PHASE[t], 1, h_all.at[pl.ds(0, G - 1), :, tile_at(t)])
+        hartree = grid_values(h_all, r)
+        mixed.append(right(fields[plane, :] + hartree * packed[plane, :], lane_minus[...]))
+        xc_part[plane, :] += hartree
+    result = left_complex(b_minus, jnp.concatenate(mixed, axis=1))
     for b in range(PL):
         for r in range(PL):
             for t in range(3):
@@ -432,7 +469,7 @@
                 ]
         space_send(8 + b, part_chunk(send2, b), part_chunk(recv2, b))
         keep(send2, recv2, b * S * CELL, CELL)
-    potential = hartree + xc_part[...]
+    potential = xc_part[...]
     for r in range(PL):
         pot_ref[r] = jnp.concatenate(
             [potential[r * N : (r + 1) * N, t * 128 : t * 128 + TILE] for t in range(3)], axis=1
@@ -492,7 +529,7 @@
             return carry
 
         for n in range(blocks):
-            lax.fori_loop(n * per_block, (n + 1) * per_block, one, 0, unroll=2)
+            lax.fori_loop(n * per_block, (n + 1) * per_block, one, 0, unroll=4)
             if b == PL - 1:
                 band_send(
                     11 + n,
@@ -582,26 +619,48 @@
     for slot in range(4):
         row = jnp.where(lane == slot, partial[slot], row)
     sum_send1[0] = row
-    band_send(20, lambda peer: sum_send1.at[0], lambda mine: sum_recv1.at[mine])
-    sum_recv1[group] = sum_send1[0]
-    wait(20, 1, sum_recv1.at[pl.ds(0, G - 1)])
+    here_low = lax.rem(me, LOW)
+    here_high = me // LOW
+    for step in range(1, G * LOW):
+        peer_band = lax.rem(group + step // LOW, G)
+        peer_low = lax.rem(here_low + step % LOW, LOW)
+        pltpu.make_async_remote_copy(
+            src_ref=sum_send1.at[0],
+            dst_ref=sum_recv1.at[group * LOW + here_low],
+            send_sem=sems.at[20, 0],
+            recv_sem=sems.at[20, 1],
+            device_id={"band": peer_band, "space": here_high * LOW + peer_low},
+            device_id_type=MESH,
+        ).start()
+    sum_recv1[group * LOW + here_low] = sum_send1[0]
+    wait(20, 1, sum_recv1.at[pl.ds(0, G * LOW - 1)])
     sum_send2[0] = jnp.sum(sum_recv1[...], axis=0)
-    space_send(21, lambda peer: sum_send2.at[0], lambda mine: sum_recv2.at[mine])
-    sum_recv2[me] = sum_send2[0]
+    for step in range(1, HIGH):
+        peer_high = lax.rem(here_high + step, HIGH)
+        pltpu.make_async_remote_copy(
+            src_ref=sum_send2.at[0],
+            dst_ref=sum_recv2.at[here_high],
+            send_sem=sems.at[21, 0],
+            recv_sem=sems.at[21, 1],
+            device_id={"space": peer_high * LOW + here_low},
+            device_id_type=MESH,
+        ).start()
+    sum_recv2[here_high] = sum_send2[0]
 
     for part in range(3):
         wait(part, 0, send1.at[every_chunk])
         wait(8 + part, 0, send2.at[every_chunk])
-    wait(3, 0, w_send.at[pl.ds(0, G - 1)])
+    for t in range(4):
+        wait(W_PHASE[t], 0, w_send.at[pl.ds(0, G - 1), :, tile_at(t)])
     wait(4, 0, h_send1.at[pl.ds(0, (S - 1) * HROWS)])
     wait(6, 0, h_send2.at[pl.ds(0, (S - 1) * HROWS)])
     wait(15, 0, over_recv.at[pl.ds(0, S - 1)])
     for n in range(blocks):
         wait(16 + n, 0, three(corr, n))
-    wait(20, 0, sum_recv1.at[pl.ds(0, G - 1)])
-
-    wait(21, 0, sum_recv2.at[pl.ds(0, S - 1)])
-    wait(21, 1, sum_recv2.at[pl.ds(0, S - 1)])
+    wait(20, 0, sum_recv1.at[pl.ds(0, G * LOW - 1)])
+
+    wait(21, 0, sum_recv2.at[pl.ds(0, HIGH - 1)])
+    wait(21, 1, sum_recv2.at[pl.ds(0, HIGH - 1)])
     row = jnp.sum(sum_recv2[...], axis=0)
 
     def pick(slot):
@@ -677,10 +736,10 @@
             band_waves,
             band_waves,
             pltpu.VMEM((1, 1, 128), F32),
-            pltpu.VMEM((G, 1, 128), F32),
+            pltpu.VMEM((G * LOW, 1, 128), F32),
             pltpu.VMEM((1, 1, 128), F32),
-            pltpu.VMEM((S, 1, 128), F32),
-            pltpu.SemaphoreType.DMA((22, 2)),
+            pltpu.VMEM((HIGH, 1, 128), F32),
+            pltpu.SemaphoreType.DMA((28, 2)),
             pltpu.SemaphoreType.DMA((len(later),)),
         ],
         compiler_params=pltpu.CompilerParams(

time: 153 us -> 155 us (1.013)
  Pallas kernels: 151 us -> 153 us
    pallas_call x1, Pallas kernels: 149 us -> 150 us  [per_device(): pl.pallas_call(body, out_shape=(waves, jax.ShapeDtypeStruct((1, 128), F32...]
where the time goes in v5:
time: 155 us; the launch traced here: 154 us
  Pallas kernels  153 us (99%)
  between operations  1.93 us (1%)
    pallas_call x1, Pallas kernels, per_device(): pl.pallas_call(body, out_shape=(waves, jax.ShapeDtypeStruct((1, 128), F32...  150 us

profile of v5, /device:TPU:1, one launch (start us, length us, event | category | flops | bytes accessed | tf_op | source)
XLA Modules:
  0.0 154.5 jit_solution(170429100548452521)
XLA Ops:
  1.9 150.4 %shard_map.202 = (f32[2,1,16384]{2,1,0:T(1,128)}, f32[1,128]{1,0:T(1,128)}, f32[3,192,192]{2,1,0:T(8,128)}) custom-call(f32[2,1,16384]{2,1,0:T(1,128)} %now_ref.1, s32[3,16384]{1,0:T(4,128)} %refs_1_.1, f32[2,1,16384]{2,1,0:T(1,128)} %refs_2_.1, f32[2,1,3,192,192]{4,3,2,1,0:T(8,128)} %refs_3_.1, f32[2,16,16384]{2,1,0:T(8,128)} %refs_4_.1, ...), custom_call_target="tpu_custom_call" | custom-call | tf_op jit(solution)/shard_map/pallas_call | solution.py:708
  152.4 2.1 %shard_map.203 = (f32[2,1,16384]{2,1,0:T(1,128)}, f32[1,2]{1,0:T(1,128)}, f32[3,192,192]{2,1,0:T(8,128)}) custom-call(f32[2,1,16384]{2,1,0:T(1,128)} %get-tuple-element.6.rest_ref, f32[2,1,16384]{2,1,0:T(1,128)} %now_ref.1, f32[1,128]{1,0:T(1,128)} %get-tuple-element.7.scalars_ref, f32[3,192,192]{2,1,0:T(8,128)} %get-tuple-element.8.pot_in), custom_call_target="tpu_custom_call" | custom-call | tf_op jit(solution)/shard_map/pallas_call | solution.py:749

commit v6 on v5

--- a/solution.py
+++ b/solution.py
@@ -28,7 +28,8 @@
 TILE = 64
 WAVES = 16384
 PLACE = 2048
-READ = 256
+READ = 1024
+PASSES = ((0, 1), (1, 3))
 BLOCK = 4096
 W_PHASE = (3, 22, 23, 24)
 H_PHASE = (7, 25, 26, 27)
@@ -477,9 +478,13 @@
 
     energy = energy_ref[0:1].reshape(1, 1)
 
-    def read_waves(b, columns):
-        seen = hot[b * N : (b + 1) * N, columns]
-        found = jnp.dot(table[...], seen, preferred_element_type=F32)
+    def read_waves(first, last, columns):
+        seen = hot[first * N : last * N, columns]
+        found = jnp.dot(
+            table[:, 0 : 2 * (last - first) * N],
+            jnp.concatenate([seen, seen], axis=0),
+            preferred_element_type=F32,
+        )
         mask = lax.broadcasted_iota(jnp.int32, (N, READ), 0) == miller_ref[2:3, columns]
         sums = []
         for half in range(2):
@@ -488,18 +493,16 @@
                 at = t * 128 + half * TILE
                 kept = jnp.where(
                     mask[t * TILE : (t + 1) * TILE],
-                    found[at : at + TILE] + found[384 + at : 384 + at + TILE],
+                    found[at : at + TILE],
                     0.0,
                 )
                 total = kept if total is None else total + kept
             sums.append(jnp.sum(total, axis=0, keepdims=True))
-        if b > 0:
+        if first > 0:
             sums = [sums[half] + lifted[group, half : half + 1, columns] for half in range(2)]
-        if b == PL - 1:
-            first = signed(miller_ref[0:1, columns])
-            second = signed(miller_ref[1:2, columns])
-            third = signed(miller_ref[2:3, columns])
-            squared = first * first + second * second + third * third
+        if last == PL:
+            index = [signed(miller_ref[d : d + 1, columns]) for d in range(3)]
+            squared = index[0] * index[0] + index[1] * index[1] + index[2] * index[2]
             diagonal = KINETIC * squared.astype(F32) / float(N * N) - energy
             sums = [sums[half] + diagonal * now_ref[half, 0:1, columns] for half in range(2)]
         for half in range(2):
@@ -511,26 +514,32 @@
     def block(ref, at, n):
         return ref.at[at, :, pl.ds(n * BLOCK, BLOCK)]
 
-    for b in range(PL):
-        wait(8 + b, 1, recv2.at[every_chunk])
-        values = jnp.concatenate(
-            [
-                jnp.concatenate([recv2[cell_rows(b, r * PL + t), :] for t in range(3)], axis=1)
-                for r in range(PL)
-            ],
-            axis=0,
-        )
-        result = left_complex(a_minus, values)
-        high = result.astype(BF16).astype(F32)
-        table[...] = jnp.transpose(jnp.concatenate([high, result - high], axis=1)).astype(BF16)
+    for first, last in PASSES:
+        highs, lows = [], []
+        for b in range(first, last):
+            wait(8 + b, 1, recv2.at[every_chunk])
+            values = jnp.concatenate(
+                [
+                    jnp.concatenate([recv2[cell_rows(b, r * PL + t), :] for t in range(3)], axis=1)
+                    for r in range(PL)
+                ],
+                axis=0,
+            )
+            result = left_complex(a_minus, values)
+            high = result.astype(BF16).astype(F32)
+            highs.append(high)
+            lows.append(result - high)
+        table[:, 0 : 2 * (last - first) * N] = jnp.transpose(
+            jnp.concatenate(highs + lows, axis=0)
+        ).astype(BF16)
 
         def one(step, carry):
-            read_waves(b, columns_at(step, READ))
+            read_waves(first, last, columns_at(step, READ))
             return carry
 
         for n in range(blocks):
-            lax.fori_loop(n * per_block, (n + 1) * per_block, one, 0, unroll=4)
-            if b == PL - 1:
+            lax.fori_loop(n * per_block, (n + 1) * per_block, one, 0, unroll=2)
+            if last == PL:
                 band_send(
                     11 + n,
                     lambda peer: block(lifted, group, n),
@@ -729,7 +738,7 @@
             narrow,
             wide,
             wide,
-            pltpu.VMEM((768, N), BF16),
+            pltpu.VMEM((384, 4 * N), BF16),
             band_waves,
             pltpu.VMEM((1, 1, 128), F32),
             pltpu.VMEM((S, 1, 128), F32),

time: 155 us -> 146 us (0.942)
  Pallas kernels: 153 us -> 143 us
    pallas_call x1, Pallas kernels: 150 us -> 141 us  [per_device(): pl.pallas_call(body, out_shape=(waves, jax.ShapeDtypeStruct((1, 128), F32...]
where the time goes in v6:
time: 146 us; the launch traced here: 145 us
  Pallas kernels  143 us (98%)
  between operations  1.93 us (1%)
    pallas_call x1, Pallas kernels, per_device(): pl.pallas_call(body, out_shape=(waves, jax.ShapeDtypeStruct((1, 128), F32...  141 us

profile of v6, /device:TPU:1, one launch (start us, length us, event | category | flops | bytes accessed | tf_op | source)
XLA Modules:
  0.0 145.4 jit_solution(2362431439931824533)
XLA Ops:
  1.9 141.4 %shard_map.202 = (f32[2,1,16384]{2,1,0:T(1,128)}, f32[1,128]{1,0:T(1,128)}, f32[3,192,192]{2,1,0:T(8,128)}) custom-call(f32[2,1,16384]{2,1,0:T(1,128)} %now_ref.1, s32[3,16384]{1,0:T(4,128)} %refs_1_.1, f32[2,1,16384]{2,1,0:T(1,128)} %refs_2_.1, f32[2,1,3,192,192]{4,3,2,1,0:T(8,128)} %refs_3_.1, f32[2,16,16384]{2,1,0:T(8,128)} %refs_4_.1, ...), custom_call_target="tpu_custom_call" | custom-call | tf_op jit(solution)/shard_map/pallas_call | solution.py:717
  143.3 2.1 %shard_map.203 = (f32[2,1,16384]{2,1,0:T(1,128)}, f32[1,2]{1,0:T(1,128)}, f32[3,192,192]{2,1,0:T(8,128)}) custom-call(f32[2,1,16384]{2,1,0:T(1,128)} %get-tuple-element.6.rest_ref, f32[2,1,16384]{2,1,0:T(1,128)} %now_ref.1, f32[1,128]{1,0:T(1,128)} %get-tuple-element.7.scalars_ref, f32[3,192,192]{2,1,0:T(8,128)} %get-tuple-element.8.pot_in), custom_call_target="tpu_custom_call" | custom-call | tf_op jit(solution)/shard_map/pallas_call | solution.py:758

commit v7 on v5

--- a/solution.py
+++ b/solution.py
@@ -28,7 +28,8 @@
 TILE = 64
 WAVES = 16384
 PLACE = 2048
-READ = 256
+READ = 1024
+HALF = N // 2
 BLOCK = 4096
 W_PHASE = (3, 22, 23, 24)
 H_PHASE = (7, 25, 26, 27)
@@ -479,27 +480,32 @@
 
     def read_waves(b, columns):
         seen = hot[b * N : (b + 1) * N, columns]
-        found = jnp.dot(table[...], seen, preferred_element_type=F32)
-        mask = lax.broadcasted_iota(jnp.int32, (N, READ), 0) == miller_ref[2:3, columns]
-        sums = []
-        for half in range(2):
-            total = None
-            for t in range(3):
-                at = t * 128 + half * TILE
-                kept = jnp.where(
-                    mask[t * TILE : (t + 1) * TILE],
-                    found[at : at + TILE] + found[384 + at : 384 + at + TILE],
-                    0.0,
-                )
-                total = kept if total is None else total + kept
-            sums.append(jnp.sum(total, axis=0, keepdims=True))
+        third = miller_ref[2:3, columns]
+        upper = third >= HALF
+        upper_bit = jnp.where(upper, 1.0, 0.0).astype(BF16)
+        high_part = seen * upper_bit
+        low_part = seen - high_part
+        found = jnp.dot(
+            table[...],
+            jnp.concatenate([low_part, low_part, high_part, high_part], axis=0),
+            preferred_element_type=F32,
+        )
+        mask = lax.broadcasted_iota(jnp.int32, (HALF, READ), 0) == jnp.where(
+            upper, third - HALF, third
+        )
+        sums = [
+            jnp.sum(
+                jnp.where(mask, found[half * HALF : (half + 1) * HALF], 0.0),
+                axis=0,
+                keepdims=True,
+            )
+            for half in range(2)
+        ]
         if b > 0:
             sums = [sums[half] + lifted[group, half : half + 1, columns] for half in range(2)]
         if b == PL - 1:
-            first = signed(miller_ref[0:1, columns])
-            second = signed(miller_ref[1:2, columns])
-            third = signed(miller_ref[2:3, columns])
-            squared = first * first + second * second + third * third
+            index = [signed(miller_ref[d : d + 1, columns]) for d in range(3)]
+            squared = index[0] * index[0] + index[1] * index[1] + index[2] * index[2]
             diagonal = KINETIC * squared.astype(F32) / float(N * N) - energy
             sums = [sums[half] + diagonal * now_ref[half, 0:1, columns] for half in range(2)]
         for half in range(2):
@@ -520,16 +526,30 @@
             ],
             axis=0,
         )
-        result = left_complex(a_minus, values)
-        high = result.astype(BF16).astype(F32)
-        table[...] = jnp.transpose(jnp.concatenate([high, result - high], axis=1)).astype(BF16)
+        turned = jnp.transpose(left_complex(a_minus, values))
+        pieces = []
+        for side in range(2):
+            rows = []
+            for half in range(2):
+                whole = jnp.concatenate(
+                    [
+                        turned[t * 128 + half * TILE : t * 128 + (half + 1) * TILE]
+                        for t in range(3)
+                    ],
+                    axis=0,
+                )
+                rows.append(whole[side * HALF : (side + 1) * HALF])
+            rows = jnp.concatenate(rows, axis=0)
+            high = rows.astype(BF16).astype(F32)
+            pieces += [high, rows - high]
+        table[...] = jnp.concatenate(pieces, axis=1).astype(BF16)
 
         def one(step, carry):
             read_waves(b, columns_at(step, READ))
             return carry
 
         for n in range(blocks):
-            lax.fori_loop(n * per_block, (n + 1) * per_block, one, 0, unroll=4)
+            lax.fori_loop(n * per_block, (n + 1) * per_block, one, 0, unroll=2)
             if b == PL - 1:
                 band_send(
                     11 + n,
@@ -729,7 +749,7 @@
             narrow,
             wide,
             wide,
-            pltpu.VMEM((768, N), BF16),
+            pltpu.VMEM((N, 4 * N), BF16),
             band_waves,
             pltpu.VMEM((1, 1, 128), F32),
             pltpu.VMEM((S, 1, 128), F32),

time: 155 us -> 144 us (0.929)
  Pallas kernels: 153 us -> 142 us
    pallas_call x1, Pallas kernels: 150 us -> 140 us  [per_device(): pl.pallas_call(body, out_shape=(waves, jax.ShapeDtypeStruct((1, 128), F32...]
where the time goes in v7:
time: 144 us
  Pallas kernels  142 us (99%)
  between operations  1.93 us (1%)
    pallas_call x1, Pallas kernels, per_device(): pl.pallas_call(body, out_shape=(waves, jax.ShapeDtypeStruct((1, 128), F32...  140 us

profile of v7, /device:TPU:1, one launch (start us, length us, event | category | flops | bytes accessed | tf_op | source)
XLA Modules:
  0.0 144.3 jit_solution(606802149028938908)
XLA Ops:
  1.9 140.3 %shard_map.202 = (f32[2,1,16384]{2,1,0:T(1,128)}, f32[1,128]{1,0:T(1,128)}, f32[3,192,192]{2,1,0:T(8,128)}) custom-call(f32[2,1,16384]{2,1,0:T(1,128)} %now_ref.1, s32[3,16384]{1,0:T(4,128)} %refs_1_.1, f32[2,1,16384]{2,1,0:T(1,128)} %refs_2_.1, f32[2,1,3,192,192]{4,3,2,1,0:T(8,128)} %refs_3_.1, f32[2,16,16384]{2,1,0:T(8,128)} %refs_4_.1, ...), custom_call_target="tpu_custom_call" | custom-call | tf_op jit(solution)/shard_map/pallas_call | solution.py:728
  142.2 2.1 %shard_map.203 = (f32[2,1,16384]{2,1,0:T(1,128)}, f32[1,2]{1,0:T(1,128)}, f32[3,192,192]{2,1,0:T(8,128)}) custom-call(f32[2,1,16384]{2,1,0:T(1,128)} %get-tuple-element.6.rest_ref, f32[2,1,16384]{2,1,0:T(1,128)} %now_ref.1, f32[1,128]{1,0:T(1,128)} %get-tuple-element.7.scalars_ref, f32[3,192,192]{2,1,0:T(8,128)} %get-tuple-element.8.pot_in), custom_call_target="tpu_custom_call" | custom-call | tf_op jit(solution)/shard_map/pallas_call | solution.py:769

commit v8 on v7

--- a/solution.py
+++ b/solution.py
@@ -87,7 +87,7 @@
         right_table(lanes(-1.0)),
         rows(1.0, order, index),
         rows(1.0, index, order),
-        rows(-1.0, order, index),
+        np.stack([rows(-1.0, order[b * S : (b + 1) * S], index) for b in range(PL)]),
         rows(-1.0, index, order),
         right_table(cas_in),
         right_table(cas_in.T),
@@ -102,8 +102,8 @@
     return high, low
 
 
-def left(table_ref, values):
-    high, low = split(values)
+def left(table_ref, values, parts=None):
+    high, low = parts or split(values)
     rows = table_ref.shape[0] // 2
     by_high = jnp.dot(table_ref[...], high, preferred_element_type=F32)
     by_low = jnp.dot(table_ref[0:rows], low, preferred_element_type=F32)
@@ -125,9 +125,10 @@
     return jnp.concatenate(tiles, axis=1)
 
 
-def left_complex(table_ref, values):
-    both = left(table_ref, values)
-    return both[0:N] + times_i(both[N:])
+def left_complex(table_ref, values, parts=None):
+    both = left(table_ref, values, parts)
+    rows = table_ref.shape[0] // 4
+    return both[0:rows] + times_i(both[rows:])
 
 
 def signed(indices):
@@ -185,6 +186,7 @@
         send2,
         recv2,
         table,
+        occ_split,
         lifted,
         over_send,
         over_recv,
@@ -461,12 +463,13 @@
         hartree = grid_values(h_all, r)
         mixed.append(right(fields[plane, :] + hartree * packed[plane, :], lane_minus[...]))
         xc_part[plane, :] += hartree
-    result = left_complex(b_minus, jnp.concatenate(mixed, axis=1))
+    parts = split(jnp.concatenate(mixed, axis=1))
     for b in range(PL):
+        result = left_complex(b_minus.at[b], None, parts)
         for r in range(PL):
             for t in range(3):
                 send2[cell_rows(b, r * PL + t), :] = result[
-                    b * S : (b + 1) * S, (r * 3 + t) * 128 : (r * 3 + t + 1) * 128
+                    :, (r * 3 + t) * 128 : (r * 3 + t + 1) * 128
                 ]
         space_send(8 + b, part_chunk(send2, b), part_chunk(recv2, b))
         keep(send2, recv2, b * S * CELL, CELL)
@@ -501,18 +504,25 @@
             )
             for half in range(2)
         ]
-        if b > 0:
-            sums = [sums[half] + lifted[group, half : half + 1, columns] for half in range(2)]
-        if b == PL - 1:
-            index = [signed(miller_ref[d : d + 1, columns]) for d in range(3)]
-            squared = index[0] * index[0] + index[1] * index[1] + index[2] * index[2]
-            diagonal = KINETIC * squared.astype(F32) / float(N * N) - energy
-            sums = [sums[half] + diagonal * now_ref[half, 0:1, columns] for half in range(2)]
         for half in range(2):
-            lifted[group, half : half + 1, columns] = sums[half]
+            lifted[group, half : half + 1, columns] += sums[half]
 
     blocks = WAVES // BLOCK
     per_block = BLOCK // READ
+
+    for n in range(blocks):
+        columns = pl.ds(n * BLOCK, BLOCK)
+        index = [signed(miller_ref[d : d + 1, columns]) for d in range(3)]
+        squared = index[0] * index[0] + index[1] * index[1] + index[2] * index[2]
+        diagonal = KINETIC * squared.astype(F32) / float(N * N) - energy
+        for half in range(2):
+            lifted[group, half : half + 1, columns] = diagonal * now_ref[half, 0:1, columns]
+        high, low = split(
+            jnp.concatenate([occ_ref[0, :, columns], occ_ref[1, :, columns]], axis=0)
+        )
+        occ_split[0:32, columns] = high
+        occ_split[32:64, columns] = low
+        occ_split[64:96, columns] = high
 
     def block(ref, at, n):
         return ref.at[at, :, pl.ds(n * BLOCK, BLOCK)]
@@ -593,24 +603,28 @@
     over_recv[me] = over_send[0]
     wait(15, 1, over_recv.at[pl.ds(0, S - 1)])
     row_sum = jnp.sum(over_recv[...], axis=0)
-    spread = jnp.where(own_row, jnp.broadcast_to(row_sum, (16, 128)), 0.0)
-    weights = []
-    for row in range(2 * G):
-        column = jnp.sum(jnp.where(band_of == row, spread, 0.0), axis=1, keepdims=True)
-        weights.append(jnp.broadcast_to(column, (16, 128)))
+    lane = lax.broadcasted_iota(jnp.int32, (8, 128), 1)
+    line = lax.broadcasted_iota(jnp.int32, (8, 128), 0)
+    spread = jnp.where(lane // 16 == line, jnp.broadcast_to(row_sum, (8, 128)), 0.0)
+    for shift in (64, 32, 16):
+        spread = spread + pltpu.roll(spread, shift, axis=1)
+    crossed = jnp.where(
+        line % 2 == 0, -pltpu.roll(spread, 7, axis=0), pltpu.roll(spread, 1, axis=0)
+    )
+    weights = jnp.where(lane // 16 % 2 == 0, spread, crossed)
+    weights_high = weights.astype(BF16).astype(F32)
+    weights = jnp.where(lane < 64, weights_high, weights - weights_high).astype(BF16)[:, :96]
 
     def correct(step, carry):
-        columns = columns_of_tile(step)
-        occ_re = occ_ref[0, :, columns]
-        occ_im = occ_ref[1, :, columns]
+        columns = columns_at(step, READ)
+        result = jnp.dot(weights, occ_split[:, columns], preferred_element_type=F32)
         for v in range(G):
-            w_re, w_im = weights[2 * v], weights[2 * v + 1]
-            corr[v, 0:1, columns] = jnp.sum(occ_re * w_re - occ_im * w_im, axis=0, keepdims=True)
-            corr[v, 1:2, columns] = jnp.sum(occ_re * w_im + occ_im * w_re, axis=0, keepdims=True)
+            for part in range(2):
+                corr[v, part : part + 1, columns] = result[2 * v + part : 2 * v + part + 1]
         return carry
 
     for n in range(blocks):
-        lax.fori_loop(n * tiles, (n + 1) * tiles, correct, 0, unroll=4)
+        lax.fori_loop(n * per_block, (n + 1) * per_block, correct, 0, unroll=2)
         band_send(
             16 + n, lambda peer: block(corr, peer, n), lambda mine: block(corr_recv, mine, n)
         )
@@ -750,6 +764,7 @@
             wide,
             wide,
             pltpu.VMEM((N, 4 * N), BF16),
+            pltpu.VMEM((96, WAVES), BF16),
             band_waves,
             pltpu.VMEM((1, 1, 128), F32),
             pltpu.VMEM((S, 1, 128), F32),

time: 144 us -> 143 us (level)
  no operation moved by 1% of the time
where the time goes in v8:
time: 143 us
  Pallas kernels  141 us (99%)
  between operations  1.93 us (1%)
    pallas_call x1, Pallas kernels, per_device(): pl.pallas_call(body, out_shape=(waves, jax.ShapeDtypeStruct((1, 128), F32...  139 us

profile of v8, /device:TPU:1, one launch (start us, length us, event | category | flops | bytes accessed | tf_op | source)
XLA Modules:
  0.0 143.0 jit_solution(16679091045791177916)
XLA Ops:
  1.9 139.0 %shard_map.202 = (f32[2,1,16384]{2,1,0:T(1,128)}, f32[1,128]{1,0:T(1,128)}, f32[3,192,192]{2,1,0:T(8,128)}) custom-call(f32[2,1,16384]{2,1,0:T(1,128)} %now_ref.1, s32[3,16384]{1,0:T(4,128)} %refs_1_.1, f32[2,1,16384]{2,1,0:T(1,128)} %refs_2_.1, f32[2,1,3,192,192]{4,3,2,1,0:T(8,128)} %refs_3_.1, f32[2,16,16384]{2,1,0:T(8,128)} %refs_4_.1, ...), custom_call_target="tpu_custom_call" | custom-call | tf_op jit(solution)/shard_map/pallas_call | solution.py:742
  140.9 2.1 %shard_map.203 = (f32[2,1,16384]{2,1,0:T(1,128)}, f32[1,2]{1,0:T(1,128)}, f32[3,192,192]{2,1,0:T(8,128)}) custom-call(f32[2,1,16384]{2,1,0:T(1,128)} %get-tuple-element.6.rest_ref, f32[2,1,16384]{2,1,0:T(1,128)} %now_ref.1, f32[1,128]{1,0:T(1,128)} %get-tuple-element.7.scalars_ref, f32[3,192,192]{2,1,0:T(8,128)} %get-tuple-element.8.pot_in), custom_call_target="tpu_custom_call" | custom-call | tf_op jit(solution)/shard_map/pallas_call | solution.py:784
